TPU v7x, 32 devices: a whole 2x2x4 slice. The times are simulated.
32 devices in a mesh: dp: 16 (over z, y, core), seq: 2 (over x).
Axes of the slice: x: 2, y: 2, z: 4, core: 2. Of those that a mesh axis runs over, the one named last changes fastest.
Arguments:
- tokens: bfloat16 [256, 200, 512], P(('dp', 'seq')), may hold values from -6 to 6
- w_qkv: bfloat16 [512, 1536], P(('dp', 'seq')), may hold values from -0.25 to 0.25
- w_attn_out: bfloat16 [512, 512], P(('dp', 'seq')), may hold values from -2 to 2
- w_router: bfloat16 [512, 16], P(('dp', 'seq')), may hold values from -0.1875 to 0.1875
- gain_attn: bfloat16 [512], P(('dp', 'seq')), may hold values from 0.5 to 1.5
- gain_moe: bfloat16 [512], P(('dp', 'seq')), may hold values from 0.5 to 1.5
- w_expert_in: bfloat16 [16, 512, 2048], P('dp', 'seq'), may hold values from -0.25 to 0.25
- w_expert_down: bfloat16 [16, 512, 2048], P('dp', 'seq'), may hold values from -4 to 4
- key_mask: int32 [256, 200], P('dp'), may hold values from 0 to 1, as said below
- expert_choice: int32 [256, 200, 2], P(('dp', 'seq')), may hold values from 0 to 15, as said below
- slot_index: int32 [256, 200, 2], P(('dp', 'seq')), may hold values from -1 to 255, as said below
- cotangent: bfloat16 [256, 200, 512], P(('dp', 'seq')), may hold values from -6 to 6
Outputs:
- mixed_out: bfloat16 [256, 200, 512], P(('dp', 'seq'))
- grad_tokens: float32 [256, 200, 512], P(('dp', 'seq'))
- grad_w_qkv: float32 [512, 1536], P(('dp', 'seq'))
- grad_w_attn_out: float32 [512, 512], P(('dp', 'seq'))
- grad_w_router: float32 [512, 16], P(('dp', 'seq'))
- grad_gain_attn: float32 [512], P(('dp', 'seq'))
- grad_gain_moe: float32 [512], P(('dp', 'seq'))
- grad_w_expert_in: float32 [16, 512, 2048], P('dp', 'seq')
- grad_w_expert_down: float32 [16, 512, 2048], P('dp', 'seq')
Inputs may be any that keep to these rules, and one draw needn't show every extreme that they name: `key_mask`: each image's row is a run of ones from position 0 followed by zeros, with 150 ones or more; in each group of 16 images of one index of dp some image has no padding. `expert_choice`: the two choices of a token differ. `slot_index`: among the tokens of one device (its 8 images), the kept choices that name one expert have distinct slots; a choice is -1 when it is dropped.
All inputs are finite; a program needn't handle non-finite values.
Results may differ from a plain program's by a relative error of at most 0.017.
Values may be sent and summed in bfloat16 or wider, within the bound.
A program may use at most 256 MiB of HBM per device.

v0:
```python
import jax
import jax.numpy as jnp
from jax import lax
from jax.sharding import PartitionSpec as P

HEADS = 8


EPSILON = 1e-06
NEGATIVE = -1e30
HIGHEST = lax.Precision.HIGHEST


def norm_rows(values):
    centred = values - jnp.mean(values, axis=-1, keepdims=True)
    inverse = lax.rsqrt(jnp.mean(centred * centred, axis=-1, keepdims=True) + EPSILON)
    return (centred * inverse, inverse)


def norm_back(grad_hat, normed, inverse):
    return inverse * (
        grad_hat
        - jnp.mean(grad_hat, axis=-1, keepdims=True)
        - normed * jnp.mean(grad_hat * normed, axis=-1, keepdims=True)
    )


def scores_for(queries, keys_in, key_keep, score_scale):
    scores = (
        jnp.einsum("iqhd,ikhd->ihqk", queries, keys_in, preferred_element_type=jnp.float32)
        * score_scale
    )
    return jnp.where(key_keep[:, None, None, :], scores, NEGATIVE)


def body(
    tokens,
    w_qkv,
    w_attn_out,
    w_router,
    gain_attn,
    gain_moe,
    w_expert_in,
    w_expert_down,
    key_mask,
    expert_choice,
    slot_index,
    cotangent,
):
    images_dev, positions, model_width = tokens.shape
    seq_count = lax.axis_size("seq")
    token_rows = images_dev * positions
    group_images = images_dev * seq_count
    head_cols = model_width // seq_count
    head_dim = model_width // HEADS
    local_heads = head_cols // head_dim
    score_scale = head_dim ** (-0.5)
    key_keep = key_mask > 0
    full_qkv, full_out, full_router, full_gain_one, full_gain_two = (
        lax.all_gather(w_qkv, ("dp", "seq"), axis=0, tiled=True),
        lax.all_gather(w_attn_out, ("dp", "seq"), axis=0, tiled=True),
        lax.all_gather(w_router, ("dp", "seq"), axis=0, tiled=True),
        lax.all_gather(gain_attn, ("dp", "seq"), axis=0, tiled=True),
        lax.all_gather(gain_moe, ("dp", "seq"), axis=0, tiled=True),
    )
    gain_one = full_gain_one.astype(jnp.float32)
    gain_two = full_gain_two.astype(jnp.float32)
    expert_count = full_router.shape[1]
    capacity = ((token_rows * 10 + 4 * expert_count - 1) // (4 * expert_count) + 7) // 8 * 8
    inputs = tokens.astype(jnp.float32).reshape(token_rows, model_width)
    hat_one, inverse_one = norm_rows(inputs)
    normed_one = (hat_one * gain_one).astype(jnp.bfloat16)
    projected = jnp.dot(normed_one, full_qkv, preferred_element_type=jnp.float32).astype(
        jnp.bfloat16
    )
    head_input = lax.all_to_all(
        projected.reshape(images_dev, positions, 3, model_width),
        "seq",
        split_axis=3,
        concat_axis=0,
        tiled=True,
    )
    queries = head_input[:, :, 0].reshape(group_images, positions, local_heads, head_dim)
    keys_in = head_input[:, :, 1].reshape(group_images, positions, local_heads, head_dim)
    values_in = head_input[:, :, 2].reshape(group_images, positions, local_heads, head_dim)
    scores = scores_for(queries, keys_in, key_keep, score_scale)
    row_max = jnp.max(scores, axis=-1, keepdims=True)
    exps = jnp.exp(scores - row_max)
    totals = jnp.sum(exps, axis=-1, keepdims=True)
    log_total = row_max + jnp.log(totals)
    weights = (exps / totals).astype(jnp.bfloat16)
    attended = jnp.einsum(
        "ihqk,ikhd->iqhd", weights, values_in, preferred_element_type=jnp.float32
    ).astype(jnp.bfloat16)
    att_back = lax.all_to_all(
        attended.reshape(group_images, positions, head_cols),
        "seq",
        split_axis=0,
        concat_axis=2,
        tiled=True,
    )
    att_rows = att_back.reshape(token_rows, model_width)
    residual = inputs + jnp.dot(att_rows, full_out, preferred_element_type=jnp.float32)
    hat_two, inverse_two = norm_rows(residual)
    normed_two = (hat_two * gain_two).astype(jnp.bfloat16)
    logits = jnp.dot(normed_two, full_router, preferred_element_type=jnp.float32)
    router_probs = jax.nn.softmax(logits, axis=-1)
    choice_rows = expert_choice.reshape(token_rows, 2)
    slot_rows = slot_index.reshape(token_rows, 2)
    onehot_pick = (
        choice_rows[:, :, None] == jnp.arange(expert_count, dtype=jnp.int32)[None, None, :]
    ).astype(jnp.float32)
    gate_values = jnp.sum(onehot_pick * router_probs[:, None, :], axis=-1)
    target = jnp.where(slot_rows >= 0, choice_rows * capacity + slot_rows, expert_count * capacity)
    send_rows = (
        jnp.zeros((expert_count * capacity, model_width), jnp.bfloat16)
        .at[target.reshape(-1)]
        .set(jnp.repeat(normed_two, 2, axis=0), mode="drop")
    )
    arrived = lax.all_to_all(
        send_rows.reshape(expert_count, capacity, model_width),
        "dp",
        split_axis=0,
        concat_axis=1,
        tiled=True,
    )
    w_in_full, w_down_full = (
        lax.all_gather(w_expert_in, "seq", axis=1, tiled=True),
        lax.all_gather(w_expert_down, "seq", axis=1, tiled=True),
    )
    inner_rows = jnp.einsum("ecd,edf->ecf", arrived, w_in_full, preferred_element_type=jnp.float32)
    activated = jax.nn.gelu(inner_rows).astype(jnp.bfloat16)
    expert_result = jnp.einsum(
        "ecf,edf->ecd", activated, w_down_full, preferred_element_type=jnp.float32
    ).astype(jnp.bfloat16)
    returned = lax.all_to_all(expert_result, "dp", split_axis=1, concat_axis=0, tiled=True)
    paired = jnp.take(
        returned.reshape(expert_count * capacity, model_width),
        target,
        axis=0,
        mode="fill",
        fill_value=0,
    ).astype(jnp.float32)
    mixed = residual + jnp.sum(gate_values[..., None] * paired, axis=1)
    mixed_out = mixed.astype(jnp.bfloat16).reshape(images_dev, positions, model_width)
    grad_out = cotangent.astype(jnp.float32).reshape(token_rows, model_width)
    grad_gates = jnp.sum(paired * grad_out[:, None, :], axis=-1)
    grad_pair = (gate_values[..., None] * grad_out[:, None, :]).astype(jnp.bfloat16)
    grad_send = (
        jnp.zeros((expert_count * capacity, model_width), jnp.bfloat16)
        .at[target.reshape(-1)]
        .set(grad_pair.reshape(token_rows * 2, model_width), mode="drop")
    )
    grad_result = lax.all_to_all(
        grad_send.reshape(expert_count, capacity, model_width),
        "dp",
        split_axis=0,
        concat_axis=1,
        tiled=True,
    )
    w_in_back, w_down_back = (
        lax.all_gather(w_expert_in, "seq", axis=1, tiled=True),
        lax.all_gather(w_expert_down, "seq", axis=1, tiled=True),
    )
    inner_back = jnp.einsum("ecd,edf->ecf", arrived, w_in_back, preferred_element_type=jnp.float32)
    act_back = jax.nn.gelu(inner_back).astype(jnp.bfloat16)
    grad_act = jnp.einsum(
        "ecd,edf->ecf", grad_result, w_down_back, preferred_element_type=jnp.float32
    )
    gelu_pull = jax.vjp(jax.nn.gelu, inner_back)[1]
    grad_inner = gelu_pull(grad_act)[0].astype(jnp.bfloat16)
    grad_down_local = jnp.einsum(
        "ecd,ecf->edf", grad_result, act_back, preferred_element_type=jnp.float32
    )
    grad_in_local = jnp.einsum(
        "ecd,ecf->edf", arrived, grad_inner, preferred_element_type=jnp.float32
    )
    grad_arrived = jnp.einsum(
        "ecf,edf->ecd", grad_inner, w_in_back, preferred_element_type=jnp.float32
    ).astype(jnp.bfloat16)
    grad_w_expert_in, grad_w_expert_down = (
        lax.psum_scatter(
            grad_in_local.astype(jnp.bfloat16), "seq", scatter_dimension=1, tiled=True
        ).astype(jnp.float32),
        lax.psum_scatter(
            grad_down_local.astype(jnp.bfloat16), "seq", scatter_dimension=1, tiled=True
        ).astype(jnp.float32),
    )
    grad_sent_back = lax.all_to_all(grad_arrived, "dp", split_axis=1, concat_axis=0, tiled=True)
    grad_routed = jnp.sum(
        jnp.take(
            grad_sent_back.reshape(expert_count * capacity, model_width),
            target,
            axis=0,
            mode="fill",
            fill_value=0,
        ).astype(jnp.float32),
        axis=1,
    )
    grad_probs = jnp.sum(onehot_pick * grad_gates[..., None], axis=1)
    grad_logits = router_probs * (
        grad_probs - jnp.sum(grad_probs * router_probs, axis=-1, keepdims=True)
    )
    grad_router_local = jnp.einsum(
        "rd,re->de", normed_two.astype(jnp.float32), grad_logits, precision=HIGHEST
    )
    grad_routed = grad_routed + jnp.einsum(
        "re,de->rd", grad_logits, full_router.astype(jnp.float32), precision=HIGHEST
    )
    grad_gain_two = jnp.sum(grad_routed * hat_two, axis=0)
    grad_residual = grad_out + norm_back(grad_routed * gain_two, hat_two, inverse_two)
    grad_att = grad_residual.astype(jnp.bfloat16)
    grad_out_local = jnp.einsum("rd,re->de", att_rows, grad_att, preferred_element_type=jnp.float32)
    grad_att_rows = jnp.einsum(
        "re,de->rd", grad_att, full_out, preferred_element_type=jnp.float32
    ).astype(jnp.bfloat16)
    grad_heads = lax.all_to_all(
        grad_att_rows.reshape(images_dev, positions, model_width),
        "seq",
        split_axis=2,
        concat_axis=0,
        tiled=True,
    )
    grad_attended = grad_heads.reshape(group_images, positions, local_heads, head_dim)
    probs_again = jnp.exp(scores_for(queries, keys_in, key_keep, score_scale) - log_total)
    grad_values = jnp.einsum(
        "ihqk,iqhd->ikhd",
        probs_again.astype(jnp.bfloat16),
        grad_attended,
        preferred_element_type=jnp.float32,
    )
    grad_weights = jnp.einsum(
        "iqhd,ikhd->ihqk", grad_attended, values_in, preferred_element_type=jnp.float32
    )
    grad_scores = (
        probs_again * (grad_weights - jnp.sum(probs_again * grad_weights, axis=-1, keepdims=True))
    ).astype(jnp.bfloat16)
    grad_queries = (
        jnp.einsum("ihqk,ikhd->iqhd", grad_scores, keys_in, preferred_element_type=jnp.float32)
        * score_scale
    )
    grad_keys = (
        jnp.einsum("ihqk,iqhd->ikhd", grad_scores, queries, preferred_element_type=jnp.float32)
        * score_scale
    )
    grad_stack = (
        jnp.stack([grad_queries, grad_keys, grad_values], axis=2)
        .reshape(group_images, positions, 3, head_cols)
        .astype(jnp.bfloat16)
    )
    grad_projected = lax.all_to_all(grad_stack, "seq", split_axis=0, concat_axis=3, tiled=True)
    grad_qkv_rows = grad_projected.reshape(token_rows, 3 * model_width)
    grad_qkv_local = jnp.einsum(
        "rd,re->de", normed_one, grad_qkv_rows, preferred_element_type=jnp.float32
    )
    grad_normed_one = jnp.einsum(
        "re,de->rd", grad_qkv_rows, full_qkv, preferred_element_type=jnp.float32
    )
    grad_gain_one = jnp.sum(grad_normed_one * hat_one, axis=0)
    grad_inputs = grad_residual + norm_back(grad_normed_one * gain_one, hat_one, inverse_one)
    grad_w_qkv, grad_w_attn_out, grad_w_router, grad_gain_attn, grad_gain_moe = (
        lax.psum_scatter(grad_qkv_local, ("dp", "seq"), scatter_dimension=0, tiled=True),
        lax.psum_scatter(grad_out_local, ("dp", "seq"), scatter_dimension=0, tiled=True),
        lax.psum_scatter(grad_router_local, ("dp", "seq"), scatter_dimension=0, tiled=True),
        lax.psum_scatter(grad_gain_one, ("dp", "seq"), scatter_dimension=0, tiled=True),
        lax.psum_scatter(grad_gain_two, ("dp", "seq"), scatter_dimension=0, tiled=True),
    )
    return (
        mixed_out,
        grad_inputs.reshape(images_dev, positions, model_width),
        grad_w_qkv,
        grad_w_attn_out,
        grad_w_router,
        grad_gain_attn,
        grad_gain_moe,
        grad_w_expert_in,
        grad_w_expert_down,
    )


def solution(mesh):
    return jax.shard_map(
        body,
        mesh=mesh,
        in_specs=(
            P(("dp", "seq"), None, None),
            P(("dp", "seq"), None),
            P(("dp", "seq"), None),
            P(("dp", "seq"), None),
            P(("dp", "seq")),
            P(("dp", "seq")),
            P("dp", "seq", None),
            P("dp", "seq", None),
            P("dp", None),
            P(("dp", "seq"), None, None),
            P(("dp", "seq"), None, None),
            P(("dp", "seq"), None, None),
        ),
        out_specs=(
            P(("dp", "seq"), None, None),
            P(("dp", "seq"), None, None),
            P(("dp", "seq"), None),
            P(("dp", "seq"), None),
            P(("dp", "seq"), None),
            P(("dp", "seq")),
            P(("dp", "seq")),
            P("dp", "seq", None),
            P("dp", "seq", None),
        ),
        check_vma=False,
    )
```

profile of v0, /device:TPU:0, one launch (start us, length us, event | category | flops | bytes accessed | tf_op | source)
XLA Modules:
  0.0 1512.0 jit_solution(12462864654486401712)
XLA Ops:
  10.5 42.0 %all-reduce.5 = (bf16[512]{0:T(512)(128)(2,1)S(1)}, bf16[512]{0:T(512)(128)(2,1)S(1)}) all-reduce(bf16[512]{0:T(512)(128)(2,1)S(1)} %dynamic-update-slice, bf16[512]{0:T(512)(128)(2,1)S(1)} %dynamic-update-slice.1), channel_id=1, replica_groups=mesh['dp'=16,'seq'=2] {'dp','seq'}, use_global_device_ids=true, to_apply=%add | all-reduce | flops 1024 | bytes 4096
  75.8 15.0 reshape.386
  107.4 70.5 %all-to-all-done = bf16[8,200,3,512]{1,0,2,3:T(8,128)(2,1)} async-done(((bf16[8,200,3,512]{1,0,2,3:T(8,128)(2,1)}), bf16[8,200,3,512]{1,0,2,3:T(8,128)(2,1)}, u32[]{:S(2)}, u32[]{:S(2)}) %all-to-all-start) | async-done | bytes 4915232 | tf_op jit(solution)/shard_map/all_to_all | solution.py:76
  231.5 79.5 %all_gather.25 = bf16[512,512]{1,0:T(8,128)(2,1)S(1)} all-gather(bf16[16,512]{1,0:T(8,128)(2,1)S(1)} %copy-done.59), channel_id=1, replica_groups=mesh['dp'=16,'seq'=2] {'dp','seq'}, dimensions={0}, use_global_device_ids=true | all-gather | bytes 540672 | tf_op jit(solution)/shard_map/all_gather | solution.py:61
  318.2 15.4 %broadcast_in_dim.39 = bf16[1600,2,512]{2,1,0:T(2,128)(2,1)} broadcast(bf16[1600,512]{1,0:T(8,128)(2,1)S(1)} %multiply_convert_fusion.7), dimensions={0,2} | broadcast | bytes 4915200 | tf_op jit(solution)/shard_map/broadcast_in_dim | solution.py:118
  341.3 20.9 %scatter_custom_fusion = bf16[4096,512]{1,0:T(8,128)(2,1)} fusion(s32[3200]{0:T(1024)S(1)} %fusion.42, bf16[3200,512]{1,0:T(8,128)(2,1)} %reshape.358, bf16[]{:T(256)} %constant.16.clone.1), kind=kCustom, calls=%fused_computation.75 | custom fusion | bytes 4194816 | tf_op jit(solution)/shard_map/scatter | solution.py:118
  367.1 15.5 %mul.285 = f32[1600,2,512]{2,1,0:T(2,128)} broadcast(bf16[1600,512]{1,0:T(8,128)(2,1)S(1)} %bitcast.142), dimensions={0,2} | broadcast | bytes 8192000 | tf_op jit(solution)/shard_map/mul | solution.py:148
  391.3 106.9 %all_gather.27 = bf16[512,16]{1,0:T(8,128)(2,1)S(1)} all-gather(bf16[16,16]{1,0:T(8,128)(2,1)S(1)} %copy-done.62), channel_id=1, replica_groups=mesh['dp'=16,'seq'=2] {'dp','seq'}, dimensions={0}, use_global_device_ids=true | all-gather | bytes 16896 | tf_op jit(solution)/shard_map/all_gather | solution.py:62
  500.8 29.9 %scatter_custom_fusion.1 = bf16[4096,512]{1,0:T(8,128)(2,1)} fusion(s32[3200]{0:T(1024)S(1)} %fusion.42, f32[3200,512]{1,0:T(8,128)} %mul.286, f32[3200]{0:T(1024)S(1)} %mul.283, bf16[]{:T(256)} %constant.16.clone.1), kind=kCustom, calls=%fused_computation.45 | custom fusion | flops 3276800 | bytes 10764290 | tf_op jit(solution)/shard_map/scatter | solution.py:152
  543.4 34.2 %all-gather.6.cloned.1.call-done = bf16[1,512,2048]{2,1,0:T(8,128)(2,1)} async-done(((bf16[1,256,2048]{2,1,0:T(8,128)(2,1)}), bf16[1,512,2048]{2,1,0:T(8,128)(2,1)}) %all-gather.6.cloned.1.call-update) | async-done | bytes 2097168 | tf_op jit(solution)/shard_map/all_gather | solution.py:128
  577.6 23.8 %multiply_convert_fusion = (bf16[4096,2048]{1,0:T(8,128)(2,1)}, f32[4096,2048]{1,0:T(8,128)}) fusion(bf16[4096,512]{1,0:T(8,128)(2,1)} %bitcast.12, bf16[1,512,2048]{2,1,0:T(8,128)(2,1)} %all-gather.6.cloned.1.call-done), kind=kOutput, calls=%fused_computation.13 | convolution fusion | flops 8665432064 | bytes 56623104 | tf_op jit(solution)/shard_map/ecd,edf->ecf/dot_general | solution.py:131
  619.9 32.4 %fusion.6 = bf16[4096,2048]{1,0:T(8,128)(2,1)} fusion(f32[4096,2048]{1,0:T(8,128)} %get-tuple-element.35, bf16[4096,512]{1,0:T(8,128)(2,1)} %bitcast.20, bf16[1,512,2048]{2,1,0:T(8,128)(2,1)} %all-gather.8.cloned.1.call-done), kind=kOutput, calls=%fused_computation.12 | convolution fusion | flops 8757706752 | bytes 56623104 | tf_op jit(solution)/shard_map/ecd,edf->ecf/dot_general | solution.py:167
  665.0 36.5 %copy.207 = bf16[1,4096,512]{2,0,1:T(2,128)(2,1)} copy(bf16[1,4096,512]{2,1,0:T(8,128)(2,1)S(1)} %fusion.16) | data formatting | bytes 8388608 | tf_op jit(solution)/shard_map/convert_element_type | solution.py:180
  702.0 28.5 %reduce.5 = bf16[4096,512]{1,0:T(8,128)(2,1)} reduce(bf16[4096,1,512]{2,1,0:T(2,128)(2,1)} %bitcast.125, bf16[]{:T(256)} %broadcast.236), dimensions={1}, to_apply=%bitcast.113.reduce_sub_computation | reduce | bytes 8388610
  742.0 20.2 %all-to-all-start.5 = ((bf16[16,2,65536]{2,1,0:T(2,128)(2,1)}), bf16[16,2,65536]{2,1,0:T(2,128)(2,1)}, u32[]{:S(2)}, u32[]{:S(2)}) async-start(bf16[16,2,65536]{2,1,0:T(2,128)(2,1)} %reshape.394), calls=%async_computation.5 | async-start | bytes 8388608 | tf_op jit(solution)/shard_map/all_to_all | solution.py:189
  774.8 36.5 %copy.208 = bf16[1,4096,512]{2,0,1:T(2,128)(2,1)} copy(bf16[1,4096,512]{2,1,0:T(8,128)(2,1)S(1)} %fusion.15) | data formatting | bytes 8388608 | tf_op jit(solution)/shard_map/convert_element_type | solution.py:135
  811.2 28.5 %reduce.4 = bf16[4096,512]{1,0:T(8,128)(2,1)} reduce(bf16[4096,1,512]{2,1,0:T(2,128)(2,1)} %bitcast.126, bf16[]{:T(256)} %broadcast.236), dimensions={1}, to_apply=%bitcast.114.reduce_sub_computation | reduce | bytes 8388610
  913.9 23.4 %all-to-all-done.3 = bf16[16,2,65536]{2,1,0:T(2,128)(2,1)} async-done(((bf16[16,2,65536]{2,1,0:T(2,128)(2,1)}), bf16[16,2,65536]{2,1,0:T(2,128)(2,1)}, u32[]{:S(2)}, u32[]{:S(2)}) %all-to-all-start.3) | async-done | bytes 4194336 | tf_op jit(solution)/shard_map/all_to_all | solution.py:136
  972.3 29.8 %fusion.10 = (f32[1600,2]{1,0:T(8,128)}, f32[1600,512]{1,0:T(8,128)}, f32[1600,512]{1,0:T(8,128)}) fusion(f32[1600,512]{1,0:T(8,128)} %convert.19, bf16[1600,2,512]{2,1,0:T(2,128)(2,1)} %reshape.381, pred[1600,2]{1,0:T(8,128)(4,1)} %copy.173, f32[1600,2]{1,0:T(8,128)} %copy-done.18, bf16[1600,2,512]{2,1,0:T(2,128)(2,1)} %reshape.385), kind=kLoop, calls=%fused_computation.26 | loop fusion | flops 13104000 | bytes 16412800 | tf_op jit(solution)/shard_map/reduce_sum | solution.py:147
  1023.9 15.0 fusion.19
  1120.4 49.1 %all-to-all-done.7 = bf16[16,200,3,256]{3,1,2,0:T(8,128)(2,1)} async-done(((bf16[16,200,3,256]{3,1,2,0:T(8,128)(2,1)}), bf16[16,200,3,256]{3,1,2,0:T(8,128)(2,1)}, u32[]{:S(2)}, u32[]{:S(2)}) %all-to-all-start.7) | async-done | bytes 4915232 | tf_op jit(solution)/shard_map/all_to_all | solution.py:251
  1211.6 55.8 %all-reduce.4 = (f32[512]{0:T(512)S(1)}, f32[512]{0:T(512)S(1)}) all-reduce(f32[512]{0:T(512)S(1)} %get-tuple-element.14, f32[512]{0:T(512)S(1)} %copy-done.61), channel_id=5, replica_groups=mesh['dp'=16,'seq'=2] {'dp','seq'}, use_global_device_ids=true, to_apply=%region_25.27.clone | all-reduce | flops 1024 | bytes 8192
  1273.4 127.7 %reduce-scatter.8.cloned.1.call-done = f32[16,512]{1,0:T(8,128)} async-done(((f32[512,512]{1,0:T(8,128)}), f32[16,512]{1,0:T(8,128)}) %reduce-scatter.8.cloned.1.call-update) | async-done | bytes 32784 | tf_op jit(solution)/shard_map/reduce_scatter | solution.py:263
  1401.0 103.3 %reduce-scatter.6.cloned.1.call-done = f32[16,1536]{1,0:T(8,128)} async-done(((f32[512,1536]{1,0:T(8,128)}), f32[16,1536]{1,0:T(8,128)}) %reduce-scatter.6.cloned.1.call-update) | async-done | bytes 98320 | tf_op jit(solution)/shard_map/reduce_scatter | solution.py:262
  (275 shorter events, 454.9 us)
Async XLA Ops:
  8.0 61.6 %copy-start.4 = (bf16[8,200,512]{2,1,0:T(8,128)(2,1)S(1)}, bf16[8,200,512]{2,1,0:T(8,128)(2,1)}, u32[]{:S(2)}) copy-start(bf16[8,200,512]{2,1,0:T(8,128)(2,1)} %param.14) | copy-start | bytes 4915204
  8.0 61.5 %all-gather.4.cloned.1.call-start = ((), (), s32[]{:S(2)}) async-start(), calls=%async_computation.13 | async-start | bytes 1622016 | tf_op jit(solution)/shard_map/all_gather | solution.py:60
  100.4 77.5 %all-to-all-start = ((bf16[8,200,3,512]{1,0,2,3:T(8,128)(2,1)}), bf16[8,200,3,512]{1,0,2,3:T(8,128)(2,1)}, u32[]{:S(2)}, u32[]{:S(2)}) async-start(bf16[8,200,3,512]{1,0,2,3:T(8,128)(2,1)} %copy.161), calls=%async_computation | async-start | bytes 12582912 | tf_op jit(solution)/shard_map/all_to_all | solution.py:76
  225.8 85.3 %all-to-all-start.1 = ((bf16[16,200,256]{2,1,0:T(8,128)(2,1)}), bf16[16,200,256]{2,1,0:T(8,128)(2,1)}, u32[]{:S(2)}, u32[]{:S(2)}) async-start(bf16[16,200,256]{2,1,0:T(8,128)(2,1)} %copy.168), calls=%async_computation.1 | async-start | bytes 3276800 | tf_op jit(solution)/shard_map/all_to_all | solution.py:95
  230.6 86.1 %copy-start.55 = (f32[512]{0:T(512)}, f32[512]{0:T(512)S(1)}, u32[]{:S(2)}) copy-start(f32[512]{0:T(512)S(1)} %convert_element_type.108) | copy-start | bytes 6148
  318.2 180.0 %copy-start.8 = (bf16[1600,512]{1,0:T(8,128)(2,1)}, bf16[1600,512]{1,0:T(8,128)(2,1)S(1)}, u32[]{:S(2)}) copy-start(bf16[1600,512]{1,0:T(8,128)(2,1)S(1)} %multiply_convert_fusion.7) | copy-start | bytes 4915204
  362.2 168.5 %all-to-all-start.2 = ((bf16[16,256,512]{2,1,0:T(8,128)(2,1)}), bf16[16,256,512]{2,1,0:T(8,128)(2,1)}, u32[]{:S(2)}, u32[]{:S(2)}) async-start(bf16[16,256,512]{2,1,0:T(8,128)(2,1)} %bitcast.141), calls=%async_computation.2 | async-start | bytes 8388608 | tf_op jit(solution)/shard_map/all_to_all | solution.py:120
  367.0 131.8 %copy-start.34 = (s32[1600,2]{0,1:T(2,128)}, s32[1600,2]{0,1:T(2,128)S(1)}, u32[]{:S(2)}) copy-start(s32[1600,2]{0,1:T(2,128)S(1)} %eq.15) | copy-start | bytes 38404
  530.7 89.2 %all-to-all-start.4 = ((bf16[16,256,512]{2,1,0:T(8,128)(2,1)}), bf16[16,256,512]{2,1,0:T(8,128)(2,1)}, u32[]{:S(2)}, u32[]{:S(2)}) async-start(bf16[16,256,512]{2,1,0:T(8,128)(2,1)} %bitcast.140), calls=%async_computation.4 | async-start | bytes 8388608 | tf_op jit(solution)/shard_map/all_to_all | solution.py:154
  542.3 35.3 %all-gather.6.cloned.1.call-start = ((), (), s32[]{:S(2)}) async-start(), calls=%async_computation.14 | async-start | bytes 3145728 | tf_op jit(solution)/shard_map/all_gather | solution.py:128
  542.8 69.2 %all-gather.8.cloned.1.call-start = ((), (), s32[]{:S(2)}) async-start(), calls=%async_computation.15 | async-start | bytes 3145728 | tf_op jit(solution)/shard_map/all_gather | solution.py:129
  619.9 32.4 %copy-start.64 = (bf16[1,512,2048]{2,1,0:T(8,128)(2,1)S(1)}, bf16[1,512,2048]{2,1,0:T(8,128)(2,1)}, u32[]{:S(2)}) copy-start(bf16[1,512,2048]{2,1,0:T(8,128)(2,1)} %all-gather.6.cloned.1.call-done) | copy-start | bytes 6291460
  742.0 109.2 %all-to-all-start.5 = ((bf16[16,2,65536]{2,1,0:T(2,128)(2,1)}), bf16[16,2,65536]{2,1,0:T(2,128)(2,1)}, u32[]{:S(2)}, u32[]{:S(2)}) async-start(bf16[16,2,65536]{2,1,0:T(2,128)(2,1)} %reshape.394), calls=%async_computation.5 | async-start | bytes 8388608 | tf_op jit(solution)/shard_map/all_to_all | solution.py:189
  851.1 86.1 %all-to-all-start.3 = ((bf16[16,2,65536]{2,1,0:T(2,128)(2,1)}), bf16[16,2,65536]{2,1,0:T(2,128)(2,1)}, u32[]{:S(2)}, u32[]{:S(2)}) async-start(bf16[16,2,65536]{2,1,0:T(2,128)(2,1)} %reshape.392), calls=%async_computation.3 | async-start | bytes 8388608 | tf_op jit(solution)/shard_map/all_to_all | solution.py:136
  859.6 338.8 %reduce-scatter.14.cloned.1.call-start = ((), (), s32[]{:S(2)}) async-start(), calls=%async_computation.20 | async-start | bytes 3145728 | tf_op jit(solution)/shard_map/reduce_scatter | solution.py:185
  972.3 32.6 %copy-start.24 = (f32[1600,16]{0,1:T(8,128)S(1)}, f32[1600,16]{0,1:T(8,128)}, u32[]{:S(2)}) copy-start(f32[1600,16]{0,1:T(8,128)} %copy-done.23) | copy-start | bytes 307204
  972.3 33.4 %copy-start.2 = (f32[1600,512]{1,0:T(8,128)S(1)}, f32[1600,512]{1,0:T(8,128)}, u32[]{:S(2)}) copy-start(f32[1600,512]{1,0:T(8,128)} %copy-done.1) | copy-start | bytes 9830404
  972.3 33.4 %copy-start.26 = (f32[1600,16]{0,1:T(8,128)S(1)}, f32[1600,16]{0,1:T(8,128)}, u32[]{:S(2)}) copy-start(f32[1600,16]{0,1:T(8,128)} %copy-done.25) | copy-start | bytes 307204
  1020.1 29.8 %all-to-all-start.6 = ((bf16[8,200,512]{1,0,2:T(8,128)(2,1)}), bf16[8,200,512]{1,0,2:T(8,128)(2,1)S(1)}, u32[]{:S(2)}, u32[]{:S(2)}) async-start(bf16[8,200,512]{1,0,2:T(8,128)(2,1)} %copy.182), calls=%async_computation.6 | async-start | bytes 4194304 | tf_op jit(solution)/shard_map/all_to_all | solution.py:217
  1023.8 177.4 %reduce-scatter.12.cloned.1.call-start = ((), (), s32[]{:S(2)}) async-start(), calls=%async_computation.19 | async-start | bytes 3145728 | tf_op jit(solution)/shard_map/reduce_scatter | solution.py:182
  1106.6 63.0 %all-to-all-start.7 = ((bf16[16,200,3,256]{3,1,2,0:T(8,128)(2,1)}), bf16[16,200,3,256]{3,1,2,0:T(8,128)(2,1)}, u32[]{:S(2)}, u32[]{:S(2)}) async-start(bf16[16,200,3,256]{3,1,2,0:T(8,128)(2,1)} %pad_maximum_fusion), calls=%async_computation.7 | async-start | bytes 9830400 | tf_op jit(solution)/shard_map/all_to_all | solution.py:251
  1112.7 160.6 %reduce-scatter.10.cloned.1.call-start = ((), (), s32[]{:S(2)}) async-start(), calls=%async_computation.18 | async-start | bytes 270336 | tf_op jit(solution)/shard_map/reduce_scatter | solution.py:264
  1115.5 285.5 %reduce-scatter.8.cloned.1.call-start = ((), (), s32[]{:S(2)}) async-start(), calls=%async_computation.17 | async-start | bytes 1081344 | tf_op jit(solution)/shard_map/reduce_scatter | solution.py:263
  1119.7 384.6 %reduce-scatter.6.cloned.1.call-start = ((), (), s32[]{:S(2)}) async-start(), calls=%async_computation.16 | async-start | bytes 3244032 | tf_op jit(solution)/shard_map/reduce_scatter | solution.py:262
  (62 other events, 517.8 us)
Sparse Core Ops, SparseCore 0:
  11.7 57.7 all-gather.3
Sparse Core Ops, SparseCore 1:
  544.3 33.3 all-gather.5
  579.0 32.9 all-gather.7
  878.7 32.1 reduce-scatter.13
  1039.0 47.1 reduce-scatter.11
  1116.3 150.1 reduce-scatter.9
  1269.4 131.5 reduce-scatter.7
  1406.9 97.4 reduce-scatter.5
where the time goes:
time: 1520 us; the launch traced here: 1510 us
  waiting for transfers between devices  452 us (30%)
  local copies, waits for them, and re-layouts  349 us (23%)
  blocking collectives  284 us (19%)
  matrix products  190 us (12%)
  other arithmetic  153 us (10%)
  starting transfers between devices  67.2 us (4%)
  between operations  16.9 us (1%)
    reduce_scatter x1, waiting for transfers between devices, body(): lax.psum_scatter(grad_out_local, ('dp', 'seq'), scatter_dimension=0, tile...  128 us
    all_gather x1, blocking collectives, body(): lax.all_gather(w_router, ('dp', 'seq'), axis=0, tiled=True)  107 us
    reduce_scatter x1, waiting for transfers between devices, body(): lax.psum_scatter(grad_qkv_local, ('dp', 'seq'), scatter_dimension=0, tile...  103 us
    unnamed x2, blocking collectives  97.8 us
    all_gather x1, blocking collectives, body(): lax.all_gather(w_attn_out, ('dp', 'seq'), axis=0, tiled=True)  79.5 us
    unnamed x156, local copies, waits for them, and re-layouts  70.7 us
    all_to_all x1, waiting for transfers between devices, body(): lax.all_to_all(projected.reshape(images_dev, positions, 3, model_width),...  70.5 us
    unnamed x3, other arithmetic  57 us
  transfers between devices with their start and end apart: 16, of which 10 were waited for; matrix products, arithmetic and copies ran while one was open for 29% of the time, Pallas kernels for 0%

commit v1 on v0

v1 whole, which is shorter than its diff:
```python
import functools

import jax
import jax.numpy as jnp
from jax import lax
from jax.experimental import pallas as pl
from jax.experimental.pallas import tpu as pltpu
from jax.sharding import PartitionSpec as P

HEADS = 8
EPSILON = 1e-06
NEGATIVE = -1e30
MESH = pl.DeviceIdType.MESH
bf16, f32 = jnp.bfloat16, jnp.float32
NN = (((1,), (0,)), ((), ()))
NT = (((1,), (1,)), ((), ()))
TN = (((0,), (0,)), ((), ()))
LANES = 128
GAIN_LANE = 64
VMEM_LIMIT = 60 << 20
Shape = jax.ShapeDtypeStruct


def dot(a, b, dims=NN):
    return lax.dot_general(a, b, dims, preferred_element_type=f32)


def pad_rows(values, rows):
    extra = rows - values.shape[0]
    if extra == 0:
        return values
    return jnp.concatenate([values, jnp.zeros((extra, values.shape[1]), values.dtype)], axis=0)


def norm_rows(values):
    centred = values - jnp.mean(values, axis=-1, keepdims=True)
    inverse = lax.rsqrt(jnp.mean(centred * centred, axis=-1, keepdims=True) + EPSILON)
    return centred * inverse, inverse


def norm_back(grad_hat, normed, inverse):
    return inverse * (
        grad_hat
        - jnp.mean(grad_hat, axis=-1, keepdims=True)
        - normed * jnp.mean(grad_hat * normed, axis=-1, keepdims=True)
    )


def router_softmax(logits, experts):
    lane = lax.broadcasted_iota(jnp.int32, logits.shape, 1)
    logits = jnp.where(lane < experts, logits, NEGATIVE)
    exps = jnp.exp(logits - jnp.max(logits, axis=1, keepdims=True))
    return exps / jnp.sum(exps, axis=1, keepdims=True)


def gelu_parts(inner):
    k, c = 0.7978845608028654, 0.044715
    square = inner * inner
    t = jnp.tanh(inner * (k + (k * c) * square))
    half = 0.5 + 0.5 * t
    value = inner * half
    slope = half + value * (1.0 - half) * (2 * k + (6 * k * c) * square)
    return value, slope


def vmem():
    return pl.BlockSpec(memory_space=pltpu.VMEM)


def anywhere():
    return pl.BlockSpec(memory_space=pl.ANY)


def per_image(*dims):
    return pl.BlockSpec((1,) + dims, lambda i: (i,) + (0,) * len(dims))


def fixed(*dims):
    return pl.BlockSpec(dims, lambda i: (0,) * len(dims))


class Layout:
    def __init__(self, dp, seq):
        self.N, self.S = dp, seq
        self.L = dp // seq

    def here(self):
        dp, s = lax.axis_index("dp"), lax.axis_index("seq")
        return dp, s, dp // self.L, lax.rem(dp, self.L)

    def member_device(self, g, m):
        return (g * self.L + m // self.S, lax.rem(m, self.S))

    def expert_of(self, g, m):
        l, s = m // self.S, lax.rem(m, self.S)
        return lax.rem(g + s + l, self.S) * self.L + l


def greet(peers):
    barrier = pltpu.get_barrier_semaphore()
    for peer in peers:
        pl.semaphore_signal(barrier, inc=1, device_id=peer, device_id_type=MESH)
    pl.semaphore_wait(barrier, len(peers))


class Rows:
    def __init__(self, dp, seq):
        self.A, self.S = dp // 4, seq

    def here(self):
        dp, s = lax.axis_index("dp"), lax.axis_index("seq")
        return dp // 4, lax.rem(dp // 2, 2), lax.rem(dp, 2), s

    def device(self, a, b, c, s):
        return ((a * 2 + b) * 2 + c, s)

    def along_a(self):
        a, b, c, s = self.here()
        return [(i, lax.rem(a + i, self.A)) for i in range(1, self.A)]

    def plane(self):
        a, b, c, s = self.here()
        for i in range(1, 2 * self.S):
            if self.S == 1:
                yield i, 1 - b, s, 0
            else:
                q = lax.rem(b * self.S + s + i, 2 * self.S)
                yield i, q // self.S, lax.rem(q, self.S), lax.rem(q, self.S)


def gather_kernel(rows, own_ref, full_ref, ssem, rsem, lsem):
    a, b, c, s = rows.here()
    sl = s if rows.S > 1 else 0
    greet(
        [rows.device(i, b, c, s) for _, i in rows.along_a()]
        + [rows.device(a, b2, c, s2) for _, b2, s2, _ in rows.plane()]
        + [rows.device(a, b, 1 - c, s)]
    )
    A, Q = rows.A, 2 * rows.S
    own = pltpu.make_async_copy(own_ref, full_ref.at[a, b, c, sl], lsem)
    own.start()
    copies = []
    for i, a2 in rows.along_a():
        copies.append(
            pltpu.make_async_remote_copy(
                own_ref, full_ref.at[a, b, c, sl], ssem.at[i], rsem.at[i],
                device_id=rows.device(a2, b, c, s), device_id_type=MESH,
            )
        )
        copies[-1].start()
    own.wait()
    for copy in copies:
        copy.wait()
    copies = []
    for i, b2, s2, _ in rows.plane():
        copies.append(
            pltpu.make_async_remote_copy(
                full_ref.at[:, b, c, sl], full_ref.at[:, b, c, sl], ssem.at[A + i], rsem.at[A + i],
                device_id=rows.device(a, b2, c, s2), device_id_type=MESH,
            )
        )
        copies[-1].start()
    for copy in copies:
        copy.wait()
    last = pltpu.make_async_remote_copy(
        full_ref.at[:, :, c], full_ref.at[:, :, c], ssem.at[A + Q], rsem.at[A + Q],
        device_id=rows.device(a, b, 1 - c, s), device_id_type=MESH,
    )
    last.start()
    last.wait()


def gather_rows(rows, own):
    height, width = own.shape
    count = rows.A + 2 * rows.S + 1
    full = pl.pallas_call(
        functools.partial(gather_kernel, rows),
        out_shape=Shape((rows.A, 2, 2, rows.S, height, width), own.dtype),
        in_specs=[vmem()],
        out_specs=vmem(),
        scratch_shapes=[
            pltpu.SemaphoreType.DMA((count,)),
            pltpu.SemaphoreType.DMA((count,)),
            pltpu.SemaphoreType.DMA,
        ],
        compiler_params=pltpu.CompilerParams(collective_id=0, has_side_effects=True, vmem_limit_bytes=VMEM_LIMIT),
    )(own)
    return full.reshape(rows.A * 4 * rows.S * height, width)


def scatter_kernel(rows, qkv_ref, out_ref, rest_ref, own_ref, part, recv1, sum1, recv2, sum2, recv3, ssem, rsem):
    a, b, c, s = rows.here()
    greet(
        [rows.device(i, b, c, s) for _, i in rows.along_a()]
        + [rows.device(a, b2, c, s2) for _, b2, s2, _ in rows.plane()]
        + [rows.device(a, b, 1 - c, s)]
    )
    A, S, Q = rows.A, rows.S, 2 * rows.S
    height = part.shape[4]
    wq, wo = qkv_ref.shape[1], out_ref.shape[1]
    for i in range(A * 4 * S):
        where = (i // (4 * S), (i // (2 * S)) % 2, (i // S) % 2, i % S)
        span = slice(i * height, (i + 1) * height)
        part[where + (slice(None), slice(0, wq))] = qkv_ref[span, :].astype(bf16)
        part[where + (slice(None), slice(wq, wq + wo))] = out_ref[span, :].astype(bf16)
        part[where + (slice(None), slice(wq + wo, None))] = rest_ref[span, :].astype(bf16)
    first = pltpu.make_async_remote_copy(
        part.at[:, :, 1 - c], recv1, ssem.at[0], rsem.at[0],
        device_id=rows.device(a, b, 1 - c, s), device_id_type=MESH,
    )
    first.start()
    first.wait()
    sum1[...] = (part[:, :, c].astype(f32) + recv1[...].astype(f32)).astype(bf16)
    copies = []
    for i, b2, s2, sl2 in rows.plane():
        copies.append(
            pltpu.make_async_remote_copy(
                sum1.at[:, b2, sl2], recv2.at[i - 1], ssem.at[i], rsem.at[i],
                device_id=rows.device(a, b2, c, s2), device_id_type=MESH,
            )
        )
        copies[-1].start()
    for copy in copies:
        copy.wait()
    sl = s if S > 1 else 0
    total = sum1[:, b, sl].astype(f32)
    for i in range(Q - 1):
        total += recv2[i].astype(f32)
    sum2[...] = total.astype(bf16)
    copies = []
    for i, a2 in rows.along_a():
        copies.append(
            pltpu.make_async_remote_copy(
                sum2.at[a2], recv3.at[i - 1], ssem.at[Q + i], rsem.at[Q + i],
                device_id=rows.device(a2, b, c, s), device_id_type=MESH,
            )
        )
        copies[-1].start()
    for copy in copies:
        copy.wait()
    final = sum2[a].astype(f32)
    for i in range(A - 1):
        final += recv3[i].astype(f32)
    own_ref[...] = final


def scatter_rows(rows, grad_qkv, grad_out, grad_rest):
    A, S = rows.A, rows.S
    width = grad_qkv.shape[1] + grad_out.shape[1] + grad_rest.shape[1]
    height = grad_qkv.shape[0] // (A * 4 * S)
    count = A + 2 * S + 1
    return pl.pallas_call(
        functools.partial(scatter_kernel, rows),
        out_shape=Shape((height, width), f32),
        in_specs=[vmem()] * 3,
        out_specs=vmem(),
        scratch_shapes=[
            pltpu.VMEM((A, 2, 2, S, height, width), bf16),
            pltpu.VMEM((A, 2, S, height, width), bf16),
            pltpu.VMEM((A, 2, S, height, width), bf16),
            pltpu.VMEM((2 * S - 1, A, height, width), bf16),
            pltpu.VMEM((A, height, width), bf16),
            pltpu.VMEM((A - 1, height, width), bf16),
            pltpu.SemaphoreType.DMA((count,)),
            pltpu.SemaphoreType.DMA((count,)),
        ],
        compiler_params=pltpu.CompilerParams(collective_id=2, has_side_effects=True, vmem_limit_bytes=VMEM_LIMIT),
    )(grad_qkv, grad_out, grad_rest)


def attend(heads, qkv, keep, width):
    head = width // heads
    outs, lses = [], []
    for h in range(heads):
        q = qkv[:, h * head : (h + 1) * head]
        k = qkv[:, width + h * head : width + (h + 1) * head]
        v = qkv[:, 2 * width + h * head : 2 * width + (h + 1) * head]
        scores = jnp.where(keep, dot(q, k, NT) * (head**-0.5), NEGATIVE)
        row_max = jnp.max(scores, axis=1, keepdims=True)
        exps = jnp.exp(scores - row_max)
        totals = jnp.sum(exps, axis=1, keepdims=True)
        lses.append(row_max + jnp.log(totals))
        outs.append(dot((exps / totals).astype(bf16), v).astype(bf16))
    return jnp.concatenate(outs, axis=1), jnp.concatenate(lses, axis=1)


def forward_kernel(
    experts, tok_ref, mask_ref, pack_ref, gains_ref, qkv_ref, att_ref, res_ref, lse_ref, routed_ref, probs_ref
):
    width = tok_ref.shape[2]
    rows = qkv_ref.shape[1]
    inputs = pad_rows(tok_ref[0].astype(f32), rows)
    hat, _ = norm_rows(inputs)
    normed = (hat * gains_ref[0:1, :]).astype(bf16)
    qkv = dot(normed, pack_ref[:, 0 : 3 * width]).astype(bf16)
    qkv_ref[0] = qkv
    att, lse = attend(HEADS, qkv, mask_ref[0] > 0, width)
    att_ref[0] = att
    lse_ref[0] = lse
    residual = inputs + dot(att, pack_ref[:, 3 * width : 4 * width])
    res_ref[0] = residual
    hat, _ = norm_rows(residual)
    routed = (hat * gains_ref[1:2, :]).astype(bf16)
    routed_ref[0] = routed
    probs_ref[0] = router_softmax(dot(routed, pack_ref[:, 4 * width :]), experts)


def forward(experts, rows, tokens, mask, pack, gains):
    images, positions, width = tokens.shape
    return pl.pallas_call(
        functools.partial(forward_kernel, experts),
        grid=(images,),
        out_shape=(
            Shape((images, rows, 3 * width), bf16),
            Shape((images, rows, width), bf16),
            Shape((images, rows, width), f32),
            Shape((images, rows, HEADS), f32),
            Shape((images, rows, width), bf16),
            Shape((images, rows, LANES), f32),
        ),
        in_specs=[per_image(positions, width), per_image(1, rows), vmem(), vmem()],
        out_specs=(
            per_image(rows, 3 * width),
            per_image(rows, width),
            per_image(rows, width),
            per_image(rows, HEADS),
            per_image(rows, width),
            per_image(rows, LANES),
        ),
        compiler_params=pltpu.CompilerParams(vmem_limit_bytes=VMEM_LIMIT),
        cost_estimate=pl.CostEstimate(flops=5 * 10**9, bytes_accessed=20 * 10**6, transcendentals=3 * 10**6),
    )(tokens, mask, pack, gains)


def expert_kernel(
    lay, experts, routed_ref, cot_ref, code_ref, router_ref, *refs
):
    S = lay.S
    w_refs, refs = refs[: 2 * S], refs[2 * S :]
    gx_ref, zy_ref, gate_ref, gwi_ref, gwd_ref = refs[:5]
    (w_in, w_down, cot, x_send, c_send, x_recv, c_recv, gx_send, zy_send, gate_send, gwi, gwd,
     wsem, xs, xr, cs, cr, gs, gr, zs, zr, ts, tr, lsem) = refs[5:]
    dp, s, g, l = lay.here()
    members, cap, width = x_send.shape
    me = l * S + s
    delta = lax.rem(s + l, S)
    slice_rows = w_in.shape[0] // S
    loads = []
    for j in range(S):
        first = pl.multiple_of(lax.rem(delta - j + S, S) * slice_rows, slice_rows)
        for which, target in ((0, w_in), (1, w_down)):
            loads.append(
                pltpu.make_async_copy(
                    w_refs[2 * j + which].at[0], target.at[pl.ds(first, slice_rows)], wsem.at[2 * j + which]
                )
            )
            loads[-1].start()
    greet([lay.member_device(g, jnp.bitwise_xor(me, k)) for k in range(1, members)])
    images, rows = routed_ref.shape[0], routed_ref.shape[1]
    for i in range(images):
        cot[i] = pad_rows(cot_ref[i].astype(f32), rows).astype(bf16)

    def remote(src, dst, send, recv, k):
        return pltpu.make_async_remote_copy(
            src, dst, send.at[k], recv.at[k],
            device_id=lay.member_device(g, jnp.bitwise_xor(me, k)), device_id_type=MESH,
        )

    def x_copy(k):
        return remote(x_send.at[jnp.bitwise_xor(me, k)], x_recv.at[me], xs, xr, k)

    def c_copy(k):
        return remote(c_send.at[jnp.bitwise_xor(me, k)], c_recv.at[me], cs, cr, k)

    def gx_copy(k):
        return remote(gx_send.at[jnp.bitwise_xor(me, k)], gx_ref.at[me], gs, gr, k)

    def zy_copy(k):
        return remote(zy_send.at[jnp.bitwise_xor(me, k)], zy_ref.at[me], zs, zr, k)

    def gate_copy(k):
        return remote(gate_send.at[jnp.bitwise_xor(me, k)], gate_ref.at[me], ts, tr, k)

    def dispatch(k, carry):
        m = jnp.bitwise_xor(me, k)
        slot = lax.broadcasted_iota(jnp.int32, (cap, images * rows), 0) + m * cap
        hit = (code_ref[0:1, :] == slot) | (code_ref[1:2, :] == slot)
        pick = jnp.where(hit, 1.0, 0.0).astype(bf16)
        x_send[m] = dot(pick, routed_ref[...].reshape(images * rows, width)).astype(bf16)
        c_send[m] = dot(pick, cot[...].reshape(images * rows, width)).astype(bf16)

        @pl.when(k > 0)
        def _():
            x_copy(k).start()
            c_copy(k).start()

        return carry

    lax.fori_loop(0, members, dispatch, 0)
    x_recv[me] = x_send[me]
    c_recv[me] = c_send[me]
    gwi[...] = jnp.zeros_like(gwi)
    gwd[...] = jnp.zeros_like(gwd)
    for load in loads:
        load.wait()
    mine = lay.expert_of(g, me)
    hidden = w_in.shape[1]
    chunk = min(512, hidden)

    def work(j, carry):
        ks = (2 * j, 2 * j + 1)
        ms = [jnp.bitwise_xor(me, k) for k in ks]

        @pl.when(j > 0)
        def _():
            x_copy(ks[0]).wait_recv()
            c_copy(ks[0]).wait_recv()

        x_copy(ks[1]).wait_recv()
        c_copy(ks[1]).wait_recv()
        x = jnp.concatenate([x_recv[m] for m in ms], axis=0)
        cf = jnp.concatenate([c_recv[m] for m in ms], axis=0).astype(f32)
        probs = router_softmax(dot(x, router_ref[...]), experts)
        lane = lax.broadcasted_iota(jnp.int32, probs.shape, 1)
        gate = jnp.sum(jnp.where(lane == mine, probs, 0.0), axis=1, keepdims=True)
        dy = (gate * cf).astype(bf16)
        y, gx = None, None
        for f in range(0, hidden, chunk):
            span = slice(f, f + chunk)
            value, slope = gelu_parts(dot(x, w_in[:, span]))
            act = value.astype(bf16)
            inner_grad = (dot(dy, w_down[:, span]) * slope).astype(bf16)
            y_part, gx_part = dot(act, w_down[:, span], NT), dot(inner_grad, w_in[:, span], NT)
            y = y_part if y is None else y + y_part
            gx = gx_part if gx is None else gx + gx_part
            gwd[:, span] += dot(dy, act, TN)
            gwi[:, span] += dot(x, inner_grad, TN)
        zy = (gate * y).astype(bf16)
        gxb = gx.astype(bf16)
        gate_grad = jnp.broadcast_to(jnp.sum(y * cf, axis=1, keepdims=True), (2 * cap, LANES)).T
        for q in range(2):
            gx_send[ms[q]] = gxb[q * cap : (q + 1) * cap]
            zy_send[ms[q]] = zy[q * cap : (q + 1) * cap]
            gate_send[ms[q]] = gate_grad[0:8, q * cap : (q + 1) * cap]

        @pl.when(j > 0)
        def _():
            gx_copy(ks[0]).start()
            gate_copy(ks[0]).start()
            zy_copy(ks[0]).start()

        gx_copy(ks[1]).start()
        gate_copy(ks[1]).start()
        zy_copy(ks[1]).start()
        return carry

    lax.fori_loop(0, members // 2, work, 0)
    keeps = [
        pltpu.make_async_copy(gx_send.at[me], gx_ref.at[me], lsem.at[0]),
        pltpu.make_async_copy(zy_send.at[me], zy_ref.at[me], lsem.at[1]),
        pltpu.make_async_copy(gate_send.at[me], gate_ref.at[me], lsem.at[2]),
    ]
    for keep in keeps:
        keep.start()
    for j in range(S):
        first = pl.multiple_of(lax.rem(delta - j + S, S) * slice_rows, slice_rows)
        gwi_ref[j] = gwi[pl.ds(first, slice_rows), :].astype(bf16)
        gwd_ref[j] = gwd[pl.ds(first, slice_rows), :].astype(bf16)
    for keep in keeps:
        keep.wait()

    def finish(k, carry):
        x_copy(k).wait_send()
        c_copy(k).wait_send()
        for copy in (gx_copy(k), zy_copy(k), gate_copy(k)):
            copy.wait()
        return carry

    lax.fori_loop(1, members, finish, 0)


def run_experts(lay, experts, cap, routed, cotangent, codes, router, weights):
    S, M = lay.S, lay.N
    images, rows, width = routed.shape
    hidden = weights[0].shape[-1]
    blocks = (M, cap, width)
    dma = pltpu.SemaphoreType.DMA((M,))
    return pl.pallas_call(
        functools.partial(expert_kernel, lay, experts),
        out_shape=(
            Shape(blocks, bf16),
            Shape(blocks, bf16),
            Shape((M, 8, cap), f32),
            Shape((S, width // S, hidden), bf16),
            Shape((S, width // S, hidden), bf16),
        ),
        in_specs=[vmem()] * 4 + [anywhere()] * (2 * S),
        out_specs=(anywhere(), anywhere(), vmem(), vmem(), vmem()),
        scratch_shapes=[
            pltpu.VMEM((width, hidden), bf16),
            pltpu.VMEM((width, hidden), bf16),
            pltpu.VMEM((images, rows, width), bf16),
            *[pltpu.VMEM(blocks, bf16)] * 6,
            pltpu.VMEM((M, 8, cap), f32),
            pltpu.VMEM((width, hidden), f32),
            pltpu.VMEM((width, hidden), f32),
            pltpu.SemaphoreType.DMA((2 * S,)),
            *[dma] * 10,
            pltpu.SemaphoreType.DMA((3,)),
        ],
        compiler_params=pltpu.CompilerParams(collective_id=1, has_side_effects=True, vmem_limit_bytes=VMEM_LIMIT),
    )(routed, cotangent, codes, router, *weights)


def backward_kernel(
    lay, tok_ref, mask_ref, cot_ref, code_ref, qkv_ref, att_ref, res_ref, lse_ref, routed_ref, probs_ref,
    pack_ref, gains_ref, gx_ref, gate_ref,
    gtok_ref, gqkv_ref, gout_ref, grest_ref, table, ggain,
):
    step = pl.program_id(0)
    _, _, g, _ = lay.here()
    images = pl.num_programs(0)
    members, _, cap = gate_ref.shape
    slots = members * cap
    rows, width = att_ref.shape[1], att_ref.shape[2]
    head = width // HEADS

    @pl.when(step == 0)
    def _():
        for ref in (gqkv_ref, gout_ref, grest_ref, ggain):
            ref[...] = jnp.zeros_like(ref)
        for m in range(members):
            values = gate_ref[m][0:1, :]
            high = values.astype(bf16).astype(f32)
            sub = lax.broadcasted_iota(jnp.int32, (LANES, cap), 0)
            here = sub == lay.expert_of(g, jnp.int32(m))
            span = slice(m * cap, (m + 1) * cap)
            table[0:LANES, span] = jnp.where(here, high, 0.0).astype(bf16)
            table[LANES : 2 * LANES, span] = jnp.where(here, values - high, 0.0).astype(bf16)

    code = code_ref[0]
    slot = lax.broadcasted_iota(jnp.int32, (rows, slots), 1)
    pick = jnp.where((code[:, 0:1] == slot) | (code[:, 1:2] == slot), 1.0, 0.0).astype(bf16)
    grad_routed = dot(pick, gx_ref[...].reshape(slots, width))
    both = dot(pick, table[...], NT)
    grad_probs = both[:, :LANES] + both[:, LANES:]
    probs = probs_ref[0]
    grad_logits = probs * (grad_probs - jnp.sum(grad_probs * probs, axis=1, keepdims=True))
    logit_high = grad_logits.astype(bf16)
    logit_low = (grad_logits - logit_high.astype(f32)).astype(bf16)
    router = pack_ref[:, 4 * width :]
    grad_router = dot(routed_ref[0], jnp.concatenate([logit_high, logit_low], axis=1), TN)
    grest_ref[...] += grad_router[:, :LANES] + grad_router[:, LANES:]
    grad_routed += dot(logit_high, router, NT) + dot(logit_low, router, NT)
    hat_two, inverse_two = norm_rows(res_ref[0])
    ggain[1:2, :] += jnp.sum(grad_routed * hat_two, axis=0, keepdims=True)
    grad_residual = pad_rows(cot_ref[0].astype(f32), rows) + norm_back(
        grad_routed * gains_ref[1:2, :], hat_two, inverse_two
    )
    grad_att = grad_residual.astype(bf16)
    gout_ref[...] += dot(att_ref[0], grad_att, TN)
    grad_attended = dot(grad_att, pack_ref[:, 3 * width : 4 * width], NT).astype(bf16)
    keep = mask_ref[0] > 0
    qkv, lse = qkv_ref[0], lse_ref[0]
    scale = head**-0.5
    grad_q, grad_k, grad_v = [], [], []
    for h in range(HEADS):
        q = qkv[:, h * head : (h + 1) * head]
        k = qkv[:, width + h * head : width + (h + 1) * head]
        v = qkv[:, 2 * width + h * head : 2 * width + (h + 1) * head]
        ga = grad_attended[:, h * head : (h + 1) * head]
        scores = jnp.where(keep, dot(q, k, NT) * scale, NEGATIVE)
        weights = jnp.exp(scores - lse[:, h : h + 1])
        grad_v.append(dot(weights.astype(bf16), ga, TN).astype(bf16))
        grad_weights = dot(ga, v, NT)
        row = jnp.sum(weights * grad_weights, axis=1, keepdims=True)
        grad_scores = (weights * (grad_weights - row)).astype(bf16)
        grad_q.append((dot(grad_scores, k) * scale).astype(bf16))
        grad_k.append((dot(grad_scores, q, TN) * scale).astype(bf16))
    grad_qkv = jnp.concatenate(grad_q + grad_k + grad_v, axis=1)
    hat_one, inverse_one = norm_rows(pad_rows(tok_ref[0].astype(f32), rows))
    normed = (hat_one * gains_ref[0:1, :]).astype(bf16)
    gqkv_ref[...] += dot(normed, grad_qkv, TN)
    grad_normed = dot(grad_qkv, pack_ref[:, 0 : 3 * width], NT)
    ggain[0:1, :] += jnp.sum(grad_normed * hat_one, axis=0, keepdims=True)
    grad_inputs = grad_residual + norm_back(grad_normed * gains_ref[0:1, :], hat_one, inverse_one)
    gtok_ref[0] = grad_inputs[: gtok_ref.shape[1]]

    @pl.when(step == images - 1)
    def _():
        zeros = jnp.zeros((GAIN_LANE, width), f32)
        tail = jnp.concatenate([zeros, ggain[...], zeros[: GAIN_LANE - 8]], axis=0)
        grest_ref[...] += tail.T


def backward(lay, tokens, mask, cotangent, code, qkv, att, res, lse, routed, probs, pack, gains, gx, gate):
    images, positions, width = tokens.shape
    rows = att.shape[1]
    slots = gate.shape[0] * gate.shape[2]
    return pl.pallas_call(
        functools.partial(backward_kernel, lay),
        grid=(images,),
        out_shape=(
            Shape((images, positions, width), f32),
            Shape((width, 3 * width), f32),
            Shape((width, width), f32),
            Shape((width, LANES), f32),
        ),
        in_specs=[
            per_image(positions, width),
            per_image(1, rows),
            per_image(positions, width),
            per_image(rows, 2),
            per_image(rows, 3 * width),
            per_image(rows, width),
            per_image(rows, width),
            per_image(rows, HEADS),
            per_image(rows, width),
            per_image(rows, LANES),
        ]
        + [vmem()] * 4,
        out_specs=(
            per_image(positions, width),
            fixed(width, 3 * width),
            fixed(width, width),
            fixed(width, LANES),
        ),
        scratch_shapes=[pltpu.VMEM((2 * LANES, slots), bf16), pltpu.VMEM((8, width), f32)],
        compiler_params=pltpu.CompilerParams(vmem_limit_bytes=VMEM_LIMIT),
        cost_estimate=pl.CostEstimate(flops=4 * 10**10, bytes_accessed=30 * 10**6, transcendentals=3 * 10**6),
    )(tokens, mask, cotangent, code, qkv, att, res, lse, routed, probs, pack, gains, gx, gate)


def mix_kernel(code_ref, res_ref, zy_ref, out_ref):
    members, cap, width = zy_ref.shape
    rows = res_ref.shape[1]
    code = code_ref[0]
    slot = lax.broadcasted_iota(jnp.int32, (rows, members * cap), 1)
    pick = jnp.where((code[:, 0:1] == slot) | (code[:, 1:2] == slot), 1.0, 0.0).astype(bf16)
    mixed = res_ref[0] + dot(pick, zy_ref[...].reshape(members * cap, width))
    out_ref[0] = mixed[: out_ref.shape[1]].astype(bf16)


def mix(positions, code, res, zy):
    images, rows, width = res.shape
    return pl.pallas_call(
        mix_kernel,
        grid=(images,),
        out_shape=Shape((images, positions, width), bf16),
        in_specs=[per_image(rows, 2), per_image(rows, width), vmem()],
        out_specs=per_image(positions, width),
        compiler_params=pltpu.CompilerParams(vmem_limit_bytes=VMEM_LIMIT),
        cost_estimate=pl.CostEstimate(flops=7 * 10**9, bytes_accessed=12 * 10**6, transcendentals=0),
    )(code, res, zy)


def body(
    lay, tokens, w_qkv, w_attn_out, w_router, gain_attn, gain_moe, w_expert_in, w_expert_down, key_mask,
    expert_choice, slot_index, cotangent,
):
    images, positions, width = tokens.shape
    N, S, L = lay.N, lay.S, lay.L
    experts = w_router.shape[1]
    rows = -(-positions // 16) * 16
    token_rows = images * positions
    capacity = ((token_rows * 10 + 4 * experts - 1) // (4 * experts) + 7) // 8 * 8
    dp, s, g, l = lay.here()

    def place(g, l, s):
        return (g * L + l) * S + s

    def route(j):
        pairs = []
        for gg in range(S):
            for ll in range(L):
                for ss in range(S):
                    d = (ss + j) % S
                    pairs.append((place(gg, ll, ss), place((gg - d) % S, ll, (d - ll) % S)))
        return pairs

    weights = []
    for j in range(S):
        weights.append(lax.ppermute(w_expert_in, ("dp", "seq"), route(j)))
        weights.append(lax.ppermute(w_expert_down, ("dp", "seq"), route(j)))

    height = w_qkv.shape[0]
    lane = jnp.arange(LANES, dtype=jnp.int32)[None, :]
    rest = jnp.pad(w_router, ((0, 0), (0, LANES - experts)))
    rest = jnp.where(lane == GAIN_LANE, gain_attn[:, None], jnp.where(lane == GAIN_LANE + 1, gain_moe[:, None], rest))
    own = jnp.concatenate([w_qkv, w_attn_out, rest], axis=1)
    if height % 16:
        own = lax.all_gather(own, "seq", axis=0, tiled=True)
        carrier = Rows(N, 1)
    else:
        carrier = Rows(N, S)
    pack = gather_rows(carrier, own)
    gains = pack[:, 4 * width + GAIN_LANE : 4 * width + GAIN_LANE + 8].T.astype(f32)

    mask = lax.dynamic_slice_in_dim(key_mask, s * images, images, axis=0)
    mask = jnp.pad(mask, ((0, 0), (0, rows - positions)))[:, None, :]
    group, local = expert_choice // L, lax.rem(expert_choice, L)
    member = local * S + lax.rem(group - g - local + (L + 1) * S, S)
    code = jnp.where(slot_index >= 0, member * capacity + slot_index, -1)
    code = jnp.pad(code, ((0, 0), (0, rows - positions), (0, 0)), constant_values=-1)
    code_rows = code.reshape(images * rows, 2).T

    qkv, att, res, lse, routed, probs = forward(experts, rows, tokens, mask, pack, gains)
    router = pack[:, 4 * width :]
    gx, zy, gate, gwi, gwd = run_experts(lay, experts, capacity, routed, cotangent, code_rows, router, weights)

    sums = []
    for partial in (gwi, gwd):
        total = None
        for j in range(S):
            back = [(b, a) for a, b in route(j)]
            part = lax.ppermute(partial[j : j + 1], ("dp", "seq"), back).astype(f32)
            total = part if total is None else total + part
        sums.append(total)

    gtok, gqkv, gout, grest = backward(
        lay, tokens, mask, cotangent, code, qkv, att, res, lse, routed, probs, pack, gains, gx, gate
    )
    mixed = mix(positions, code, res, zy)
    own = scatter_rows(carrier, gqkv, gout, grest)
    if height % 16:
        own = lax.psum_scatter(own, "seq", scatter_dimension=0, tiled=True)
    rest = own[:, 4 * width :]
    return (
        mixed,
        gtok,
        own[:, : 3 * width],
        own[:, 3 * width : 4 * width],
        rest[:, :experts],
        rest[:, GAIN_LANE],
        rest[:, GAIN_LANE + 1],
        sums[0],
        sums[1],
    )


def solution(mesh):
    lay = Layout(mesh.shape["dp"], mesh.shape["seq"])
    return jax.shard_map(
        functools.partial(body, lay),
        mesh=mesh,
        in_specs=(
            P(("dp", "seq"), None, None),
            P(("dp", "seq"), None),
            P(("dp", "seq"), None),
            P(("dp", "seq"), None),
            P(("dp", "seq")),
            P(("dp", "seq")),
            P("dp", "seq", None),
            P("dp", "seq", None),
            P("dp", None),
            P(("dp", "seq"), None, None),
            P(("dp", "seq"), None, None),
            P(("dp", "seq"), None, None),
        ),
        out_specs=(
            P(("dp", "seq"), None, None),
            P(("dp", "seq"), None, None),
            P(("dp", "seq"), None),
            P(("dp", "seq"), None),
            P(("dp", "seq"), None),
            P(("dp", "seq")),
            P(("dp", "seq")),
            P("dp", "seq", None),
            P("dp", "seq", None),
        ),
        check_vma=False,
    )
```

time: 1520 us -> 610 us (0.40)
  Pallas kernels: 0 us -> 478 us
  waiting for transfers between devices: 452 us -> 56.8 us
  local copies, waits for them, and re-layouts: 349 us -> 18 us
  blocking collectives: 284 us -> 0 us
  matrix products: 190 us -> 0 us
  other arithmetic: 153 us -> 12.4 us
  starting transfers between devices: 67.2 us -> 32.4 us
  between operations: 16.9 us -> 0.88 us
    pallas_call x0 -> x6, Pallas kernels: none -> 478 us  [the longest x1 234 us: run_experts(): pl.pallas_call(functools.partial(expert_kernel, lay, experts), out_shape=...]
    reduce_scatter x5 -> x0, waiting for transfers between devices: 231 us -> none  [the longest x1 128 us: body(): lax.psum_scatter(grad_out_local, ('dp', 'seq'), scatter_dimension=0, tile...]
    dot_general x21 -> x0, matrix products: 190 us -> none  [the longest x1 32.4 us: body(): jnp.einsum('ecd,edf->ecf', grad_result, w_down_back, preferred_element_ty...]
    all_gather x2 -> x0, blocking collectives: 186 us -> none  [the longest x1 107 us: body(): lax.all_gather(w_router, ('dp', 'seq'), axis=0, tiled=True)]
    all_to_all x8 -> x0, waiting for transfers between devices: 162 us -> none  [the longest x1 70.5 us: body(): lax.all_to_all(projected.reshape(images_dev, positions, 3, model_width),...]
    unnamed x2 -> x0, blocking collectives: 97.8 us -> none
    convert_element_type x2 -> x0, local copies, waits for them, and re-layouts: 72.9 us -> none  [the longest x1 36.5 us: body(): grad_arrived = jnp.einsum('ecf,edf->ecd', grad_inner, w_in_back, preferre...]
    unnamed x156 -> x16, local copies, waits for them, and re-layouts: 70.7 us -> 2.06 us
  transfers between devices with their start and end apart: 16 -> 8, of which waited for: 10 -> 2; matrix products, arithmetic and copies ran while one was open for 29% -> 3% of each run, Pallas kernels for 0% -> 22%
where the time goes in v1:
time: 610 us; the launch traced here: 599 us
  Pallas kernels  478 us (78%)
  waiting for transfers between devices  56.8 us (9%)
  starting transfers between devices  32.4 us (5%)
  local copies, waits for them, and re-layouts  18 us (3%)
  other arithmetic  12.4 us (2%)
    pallas_call x1, Pallas kernels, run_experts(): pl.pallas_call(functools.partial(expert_kernel, lay, experts), out_shape=...  234 us
    pallas_call x1, Pallas kernels, gather_rows(): pl.pallas_call(functools.partial(gather_kernel, rows), out_shape=Shape((r...  94.9 us
    pallas_call x1, Pallas kernels, backward(): pl.pallas_call(functools.partial(backward_kernel, lay), grid=(images,), o...  80.3 us
    ppermute x4, waiting for transfers between devices, body(): part = lax.ppermute(partial[j:j + 1], ('dp', 'seq'), back).astype(f32)  56.8 us
    pallas_call x1, Pallas kernels, scatter_rows(): pl.pallas_call(functools.partial(scatter_kernel, rows), out_shape=Shape((...  30.6 us
    pallas_call x1, Pallas kernels, forward(): pl.pallas_call(functools.partial(forward_kernel, experts), grid=(images,)...  26.4 us
  transfers between devices with their start and end apart: 8, of which 2 were waited for; matrix products, arithmetic and copies ran while one was open for 3% of the time, Pallas kernels for 22%

profile of v1, /device:TPU:0, one launch (start us, length us, event | category | flops | bytes accessed | tf_op | source)
XLA Modules:
  0.0 598.6 jit_solution(14995637963367120219)
XLA Ops:
  0.7 2.0 collective-permute-start
  2.7 7.2 %collective-permute-start.2 = (bf16[1,256,2048]{2,1,0:T(8,128)(2,1)}, bf16[1,256,2048]{2,1,0:T(8,128)(2,1)}, u32[]{:S(2)}, u32[]{:S(2)}) collective-permute-start(bf16[1,256,2048]{2,1,0:T(8,128)(2,1)} %param.18), channel_id=1, source_target_pairs={{0,17},{1,0},{2,18},{3,3},{4,21},{5,4},{6,22},{7,7},{8,25},{9,8},{... | collective-permute-start | bytes 3145736 | tf_op jit(solution)/shard_map/ppermute | solution.py:683
  9.9 9.5 %collective-permute-start.1 = (bf16[1,256,2048]{2,1,0:T(8,128)(2,1)}, bf16[1,256,2048]{2,1,0:T(8,128)(2,1)}, u32[]{:S(2)}, u32[]{:S(2)}) collective-permute-start(bf16[1,256,2048]{2,1,0:T(8,128)(2,1)} %param.19), channel_id=1, source_target_pairs={{0,0},{1,17},{2,3},{3,18},{4,4},{5,21},{6,7},{7,22},{8,8},{9,25},{... | collective-permute-start | bytes 3145736 | tf_op jit(solution)/shard_map/ppermute | solution.py:684
  19.4 1.9 collective-permute-start.3
  23.9 1.5 pad_maximum_fusion.own_ref
  25.3 94.9 %shard_map.187 = bf16[4,2,2,2,16,2176]{5,4,3,2,1,0:T(8,128)(2,1)} custom-call(bf16[16,2176]{1,0:T(8,128)(2,1)} %pad_maximum_fusion.own_ref), custom_call_target="tpu_custom_call" | custom-call | tf_op jit(solution)/shard_map/pallas_call | solution.py:176
  120.3 1.7 slice.48
  122.0 1.6 slice.49.router_ref
  125.6 1.7 negate_select_fusion.3
  131.7 26.4 %shard_map.188 = (bf16[8,208,1536]{2,1,0:T(8,128)(2,1)}, bf16[8,208,512]{2,1,0:T(8,128)(2,1)}, f32[8,208,512]{2,1,0:T(8,128)}, f32[8,208,8]{2,1,0:T(8,128)}, bf1...) custom-call(bf16[8,200,512]{2,1,0:T(8,128)(2,1)} %tok_ref.3, s32[8,1,208]{2,1,0:T(1,128)} %broadcast_in_dim.34.mask_ref, ...), custom_call_target="tpu_custom_call" | custom-call | flops 5000000000 | bytes 20000000 | tf_op jit(solution)/shard_map/pallas_call | solution.py:310
  159.1 233.7 %shard_map.189 = (bf16[16,256,512]{2,1,0:T(8,128)(2,1)}, bf16[16,256,512]{2,1,0:T(8,128)(2,1)}, f32[16,8,256]{2,1,0:T(8,128)}, bf16[2,256,2048]{2,1,0:T(8,128)(2,1)}, bf16[2,256,2048]{2,1,0:T(8,128)(2,1)}) custom-call(bf16[8,208,512]{2,1,0:T(8,128)(2,1)} %get-tuple-element.25.routed_ref, bf16[8,200,512]{2,1,0:T(8,128)(2,1)} %cot_ref.3, s32[2,1664]{1,0:T(2,128)} %bitcast.10, ...), custom_call_target="tpu_custom_call" | custom-call | tf_op jit(solution)/shard_map/pallas_call | solution.py:488
  392.8 80.3 %shard_map.191 = (f32[8,200,512]{2,1,0:T(8,128)}, f32[512,1536]{1,0:T(8,128)}, f32[512,512]{1,0:T(8,128)}, f32[512,128]{1,0:T(8,128)}) custom-call(bf16[8,200,512]{2,1,0:T(8,128)(2,1)} %tok_ref.3, s32[8,1,208]{2,1,0:T(1,128)} %broadcast_in_dim.34.mask_ref, bf16[8,200,512]{2,1,0:T(8,128)(2,1)} %cot_ref.3, s32[8,208,2]{2,1,0:T(8,128)} %copy-done.1, ...), custom_call_target="tpu_custom_call" | custom-call | flops 40000000000 | bytes 30000000 | tf_op jit(solution)/shard_map/pallas_call | solution.py:600
  473.2 30.6 %shard_map.192 = f32[16,2176]{1,0:T(8,128)} custom-call(f32[512,1536]{1,0:T(8,128)} %get-tuple-element.34.qkv_ref, f32[512,512]{1,0:T(8,128)} %get-tuple-element.35.out_ref, f32[512,128]{1,0:T(8,128)} %get-tuple-element.36.rest_ref), custom_call_target="tpu_custom_call" | custom-call | tf_op jit(solution)/shard_map/pallas_call | solution.py:252
  503.7 1.5 slice.39
  509.2 2.9 collective-permute-start.5
  512.1 1.6 collective-permute-start.4
  514.8 5.6 collective-permute-start.7
  520.4 1.7 collective-permute-start.6
  522.1 1.5 slice_reduce_fusion
  523.6 12.1 %shard_map.190 = bf16[8,200,512]{2,1,0:T(8,128)(2,1)} custom-call(s32[8,208,2]{2,1,0:T(8,128)} %copy-done.1, f32[8,208,512]{2,1,0:T(8,128)} %get-tuple-element.24.res_ref, bf16[16,256,512]{2,1,0:T(8,128)(2,1)} %get-tuple-element.26.zy_ref), custom_call_target="tpu_custom_call" | custom-call | flops 7000000000 | bytes 12000000 | tf_op jit(solution)/shard_map/pallas_call | solution.py:646
  535.7 37.1 %collective-permute-done.5 = bf16[1,256,2048]{2,1,0:T(8,128)(2,1)S(1)} collective-permute-done((bf16[1,256,2048]{2,1,0:T(8,128)(2,1)}, bf16[1,256,2048]{2,1,0:T(8,128)(2,1)S(1)}, u32[]{:S(2)}, u32[]{:S(2)}) %collective-permute-start.5) | collective-permute-done | bytes 1048608 | tf_op jit(solution)/shard_map/ppermute | solution.py:716
  572.8 2.9 convert_add_fusion.1
  575.7 19.7 %collective-permute-done.7 = bf16[1,256,2048]{2,1,0:T(8,128)(2,1)} collective-permute-done((bf16[1,256,2048]{2,1,0:T(8,128)(2,1)}, bf16[1,256,2048]{2,1,0:T(8,128)(2,1)}, u32[]{:S(2)}, u32[]{:S(2)}) %collective-permute-start.7) | collective-permute-done | bytes 1048608 | tf_op jit(solution)/shard_map/ppermute | solution.py:716
  595.4 3.2 convert_add_fusion
  (43 shorter events, 14.9 us)
Async XLA Ops:
  0.6 128.7 %copy-start = (s32[16,200]{1,0:T(8,128)S(1)}, s32[16,200]{1,0:T(8,128)}, u32[]{:S(2)}) copy-start(s32[16,200]{1,0:T(8,128)} %param.20) | copy-start | bytes 38404
  0.7 122.9 %copy-start.6 = (s32[8,200,2]{1,2,0:T(2,128)S(1)}, s32[8,200,2]{1,2,0:T(2,128)}, u32[]{:S(2)}) copy-start(s32[8,200,2]{1,2,0:T(2,128)} %param.22) | copy-start | bytes 38404
  0.7 157.5 %collective-permute-start = (bf16[1,256,2048]{2,1,0:T(8,128)(2,1)}, bf16[1,256,2048]{2,1,0:T(8,128)(2,1)S(1)}, u32[]{:S(2)}, u32[]{:S(2)}) collective-permute-start(bf16[1,256,2048]{2,1,0:T(8,128)(2,1)} %param.18), channel_id=1, source_target_pairs={{0,0},{1,17},{2,3},{3,18},{4,4},{5,21},{6,7},{7,22},{8,8},{9,25},{... | collective-permute-start | bytes 3145736 | tf_op jit(solution)/shard_map/ppermute | solution.py:683
  2.7 155.5 %collective-permute-start.2 = (bf16[1,256,2048]{2,1,0:T(8,128)(2,1)}, bf16[1,256,2048]{2,1,0:T(8,128)(2,1)}, u32[]{:S(2)}, u32[]{:S(2)}) collective-permute-start(bf16[1,256,2048]{2,1,0:T(8,128)(2,1)} %param.18), channel_id=1, source_target_pairs={{0,17},{1,0},{2,18},{3,3},{4,21},{5,4},{6,22},{7,7},{8,25},{9,8},{... | collective-permute-start | bytes 3145736 | tf_op jit(solution)/shard_map/ppermute | solution.py:683
  9.9 148.2 %collective-permute-start.1 = (bf16[1,256,2048]{2,1,0:T(8,128)(2,1)}, bf16[1,256,2048]{2,1,0:T(8,128)(2,1)}, u32[]{:S(2)}, u32[]{:S(2)}) collective-permute-start(bf16[1,256,2048]{2,1,0:T(8,128)(2,1)} %param.19), channel_id=1, source_target_pairs={{0,0},{1,17},{2,3},{3,18},{4,4},{5,21},{6,7},{7,22},{8,8},{9,25},{... | collective-permute-start | bytes 3145736 | tf_op jit(solution)/shard_map/ppermute | solution.py:684
  19.4 138.8 %collective-permute-start.3 = (bf16[1,256,2048]{2,1,0:T(8,128)(2,1)}, bf16[1,256,2048]{2,1,0:T(8,128)(2,1)}, u32[]{:S(2)}, u32[]{:S(2)}) collective-permute-start(bf16[1,256,2048]{2,1,0:T(8,128)(2,1)} %param.19), channel_id=1, source_target_pairs={{0,17},{1,0},{2,18},{3,3},{4,21},{5,4},{6,22},{7,7},{8,25},{9,8},{... | collective-permute-start | bytes 3145736 | tf_op jit(solution)/shard_map/ppermute | solution.py:684
  127.9 2.2 copy-start.5
  129.4 28.8 %copy-start.1 = (s32[8,208,2]{2,1,0:T(8,128)}, s32[8,208,2]{2,1,0:T(8,128)S(1)}, u32[]{:S(2)}) copy-start(s32[8,208,2]{2,1,0:T(8,128)S(1)} %pad.12.code_ref) | copy-start | bytes 39940
  158.1 1.0 copy-start.4
  473.1 34.8 %copy-start.3 = (bf16[2,256,2048]{2,1,0:T(8,128)(2,1)S(1)}, bf16[2,256,2048]{2,1,0:T(8,128)(2,1)}, u32[]{:S(2)}) copy-start(bf16[2,256,2048]{2,1,0:T(8,128)(2,1)} %get-tuple-element.37) | copy-start | bytes 6291460
  508.0 5.8 copy-start.2
  509.2 63.6 %collective-permute-start.5 = (bf16[1,256,2048]{2,1,0:T(8,128)(2,1)}, bf16[1,256,2048]{2,1,0:T(8,128)(2,1)S(1)}, u32[]{:S(2)}, u32[]{:S(2)}) collective-permute-start(bf16[1,256,2048]{2,1,0:T(8,128)(2,1)} %get-tuple-element.44), channel_id=1, source_target_pairs={{17,0},{0,1},{18,2},{3,3},{21,4},{4,5},{22,6},{7,7},{25,8},{8,9},{... | collective-permute-start | bytes 3145736 | tf_op jit(solution)/shard_map/ppermute | solution.py:716
  512.1 60.7 %collective-permute-start.4 = (bf16[1,256,2048]{2,1,0:T(8,128)(2,1)S(1)}, bf16[1,256,2048]{2,1,0:T(8,128)(2,1)}, u32[]{:S(2)}, u32[]{:S(2)}) collective-permute-start(bf16[1,256,2048]{2,1,0:T(8,128)(2,1)S(1)} %get-tuple-element.43), channel_id=1, source_target_pairs={{0,0},{17,1},{3,2},{18,3},{4,4},{21,5},{7,6},{22,7},{8,8},{25,9},{... | collective-permute-start | bytes 3145736 | tf_op jit(solution)/shard_map/ppermute | solution.py:716
  514.8 80.6 %collective-permute-start.7 = (bf16[1,256,2048]{2,1,0:T(8,128)(2,1)}, bf16[1,256,2048]{2,1,0:T(8,128)(2,1)}, u32[]{:S(2)}, u32[]{:S(2)}) collective-permute-start(bf16[1,256,2048]{2,1,0:T(8,128)(2,1)} %get-tuple-element.42), channel_id=1, source_target_pairs={{17,0},{0,1},{18,2},{3,3},{21,4},{4,5},{22,6},{7,7},{25,8},{8,9},{... | collective-permute-start | bytes 3145736 | tf_op jit(solution)/shard_map/ppermute | solution.py:716
  520.4 75.0 %collective-permute-start.6 = (bf16[1,256,2048]{2,1,0:T(8,128)(2,1)S(1)}, bf16[1,256,2048]{2,1,0:T(8,128)(2,1)}, u32[]{:S(2)}, u32[]{:S(2)}) collective-permute-start(bf16[1,256,2048]{2,1,0:T(8,128)(2,1)S(1)} %get-tuple-element.41), channel_id=1, source_target_pairs={{0,0},{17,1},{3,2},{18,3},{4,4},{21,5},{7,6},{22,7},{8,8},{25,9},{... | collective-permute-start | bytes 3145736 | tf_op jit(solution)/shard_map/ppermute | solution.py:716

commit v2 on v1

v2 whole, which is shorter than its diff:
```python
import functools

import jax
import jax.numpy as jnp
from jax import lax
from jax.experimental import pallas as pl
from jax.experimental.pallas import tpu as pltpu
from jax.sharding import PartitionSpec as P

HEADS = 8
EPSILON = 1e-06
NEGATIVE = -1e30
MESH = pl.DeviceIdType.MESH
bf16, f32 = jnp.bfloat16, jnp.float32
NN = (((1,), (0,)), ((), ()))
NT = (((1,), (1,)), ((), ()))
TN = (((0,), (0,)), ((), ()))
LANES = 128
GAIN_LANE = 64
VMEM_LIMIT = 60 << 20
Shape = jax.ShapeDtypeStruct


def dot(a, b, dims=NN):
    return lax.dot_general(a, b, dims, preferred_element_type=f32)


def pad_rows(values, rows):
    extra = rows - values.shape[0]
    if extra == 0:
        return values
    return jnp.concatenate([values, jnp.zeros((extra, values.shape[1]), values.dtype)], axis=0)


def norm_rows(values):
    centred = values - jnp.mean(values, axis=-1, keepdims=True)
    inverse = lax.rsqrt(jnp.mean(centred * centred, axis=-1, keepdims=True) + EPSILON)
    return centred * inverse, inverse


def norm_back(grad_hat, normed, inverse):
    return inverse * (
        grad_hat
        - jnp.mean(grad_hat, axis=-1, keepdims=True)
        - normed * jnp.mean(grad_hat * normed, axis=-1, keepdims=True)
    )


def router_softmax(logits, experts):
    lane = lax.broadcasted_iota(jnp.int32, logits.shape, 1)
    logits = jnp.where(lane < experts, logits, NEGATIVE)
    exps = jnp.exp(logits - jnp.max(logits, axis=1, keepdims=True))
    return exps / jnp.sum(exps, axis=1, keepdims=True)


def gelu_parts(inner):
    k, c = 0.7978845608028654, 0.044715
    square = inner * inner
    t = jnp.tanh(inner * (k + (k * c) * square))
    half = 0.5 + 0.5 * t
    value = inner * half
    slope = half + value * (1.0 - half) * (2 * k + (6 * k * c) * square)
    return value, slope


def anywhere():
    return pl.BlockSpec(memory_space=pl.ANY)


def per_image(*dims):
    return pl.BlockSpec((1,) + dims, lambda i: (i,) + (0,) * len(dims))


def fixed(*dims):
    return pl.BlockSpec(dims, lambda i: (0,) * len(dims), pipeline_mode=pl.Buffered(1))


class Layout:
    def __init__(self, dp, seq):
        self.N, self.S = dp, seq
        self.L = dp // seq

    def here(self):
        dp, s = lax.axis_index("dp"), lax.axis_index("seq")
        return dp, s, dp // self.L, lax.rem(dp, self.L)

    def member_device(self, g, m):
        return (g * self.L + m // self.S, lax.rem(m, self.S))

    def group_peers(self):
        _, s, g, l = self.here()
        return [self.member_device(g, jnp.bitwise_xor(l * self.S + s, k)) for k in range(1, self.N)]

    def weight_peers(self):
        _, s, g, l = self.here()
        count = self.S * self.S
        places = [lax.rem(g * self.S + s + i, count) for i in range(1, count)]
        return [(q // self.S * self.L + l, lax.rem(q, self.S)) for q in places]

    def expert_of(self, g, m):
        l, s = m // self.S, lax.rem(m, self.S)
        return lax.rem(g + s + l, self.S) * self.L + l


def greet(peers):
    barrier = pltpu.get_barrier_semaphore()
    for peer in peers:
        pl.semaphore_signal(barrier, inc=1, device_id=peer, device_id_type=MESH)
    pl.semaphore_wait(barrier, len(peers))


class Rows:
    def __init__(self, dp, seq):
        self.A, self.S = dp // 4, seq

    def here(self):
        dp, s = lax.axis_index("dp"), lax.axis_index("seq")
        return dp // 4, lax.rem(dp // 2, 2), lax.rem(dp, 2), s

    def device(self, a, b, c, s):
        return ((a * 2 + b) * 2 + c, s)

    def along_a(self):
        a, b, c, s = self.here()
        return [(i, lax.rem(a + i, self.A)) for i in range(1, self.A)]

    def plane(self):
        a, b, c, s = self.here()
        for i in range(1, 2 * self.S):
            if self.S == 1:
                yield i, 1 - b, s, 0
            else:
                q = lax.rem(b * self.S + s + i, 2 * self.S)
                yield i, q // self.S, lax.rem(q, self.S), lax.rem(q, self.S)


def attend(heads, qkv, keep, width):
    head = width // heads
    outs, lses = [], []
    for h in range(heads):
        q = qkv[:, h * head : (h + 1) * head]
        k = qkv[:, width + h * head : width + (h + 1) * head]
        v = qkv[:, 2 * width + h * head : 2 * width + (h + 1) * head]
        scores = jnp.where(keep, dot(q, k, NT) * (head**-0.5), NEGATIVE)
        row_max = jnp.max(scores, axis=1, keepdims=True)
        exps = jnp.exp(scores - row_max)
        totals = jnp.sum(exps, axis=1, keepdims=True)
        lses.append(row_max + jnp.log(totals))
        outs.append(dot((exps / totals).astype(bf16), v).astype(bf16))
    return jnp.concatenate(outs, axis=1), jnp.concatenate(lses, axis=1)


def front_kernel(
    lay, rows, experts,
    own_ref, tok_ref, mask_ref, cot_ref, code_ref, w_in_ref, w_down_ref,
    pack_ref, gains_ref, qkv_ref, att_ref, res_ref, lse_ref, routed_ref, probs_ref,
    gx_ref, zy_ref, gate_ref, gwi_ref, gwd_ref,
    full, routed, cot, w_in, w_down, x_send, c_send, x_recv, c_recv, gate_send, gwi, gwd,
    ps, pr, ws, wr, xs, xr, cs, cr, gs, gr, ts, tr, zs, ls,
):
    step = pl.program_id(0)
    steps = pl.num_programs(0)
    a, b, c, s = rows.here()
    _, _, g, l = lay.here()
    S, L = lay.S, lay.L
    members, cap, width = x_send.shape
    images, height = routed.shape[0], routed.shape[1]
    me = l * S + s
    delta = lax.rem(s + l, S)
    part_rows = w_in.shape[0] // S

    def remote(src, dst, send, recv, device):
        return pltpu.make_async_remote_copy(src, dst, send, recv, device_id=device, device_id_type=MESH)

    def to_member(src, dst, send, recv, k):
        return remote(src, dst, send.at[k], recv.at[k], lay.member_device(g, jnp.bitwise_xor(me, k)))

    def x_copy(k):
        return to_member(x_send.at[jnp.bitwise_xor(me, k)], x_recv.at[me], xs, xr, k)

    def c_copy(k):
        return to_member(c_send.at[jnp.bitwise_xor(me, k)], c_recv.at[me], cs, cr, k)

    def gx_copy(k):
        return to_member(c_send.at[jnp.bitwise_xor(me, k)], gx_ref.at[me], gs, gr, k)

    def gate_copy(k):
        return to_member(gate_send.at[jnp.bitwise_xor(me, k)], gate_ref.at[me], ts, tr, k)

    def zy_copy(k):
        m = jnp.bitwise_xor(me, k)
        return pltpu.make_async_copy(x_send.at[m], zy_ref.at[m], zs.at[k])

    def pick_rows(m, values, target):
        slot = lax.broadcasted_iota(jnp.int32, (cap, images * height), 0) + m * cap
        hit = (code_ref[0:1, :] == slot) | (code_ref[1:2, :] == slot)
        pick = jnp.where(hit, 1.0, 0.0).astype(bf16)
        target[m] = dot(pick, values[...].reshape(images * height, width)).astype(bf16)

    def build_c(first, last):
        def build(k, carry):
            pick_rows(jnp.bitwise_xor(me, k), cot, c_send)
            return carry

        lax.fori_loop(first, last, build, 0)

    def weight_copies(d):
        device = (lax.rem(g - d + S, S) * L + l, lax.rem(d - l + L * S, S))
        mine = pl.ds(pl.multiple_of(s * part_rows, part_rows), part_rows)
        return [
            remote(src.at[0], dst.at[mine], ws.at[2 * d + i], wr.at[2 * s + i], device)
            for i, (src, dst) in enumerate(((w_in_ref, w_in), (w_down_ref, w_down)))
        ]

    def weight_local():
        mine = pl.ds(pl.multiple_of(s * part_rows, part_rows), part_rows)
        return [
            pltpu.make_async_copy(src.at[0], dst.at[mine], wr.at[2 * s + i])
            for i, (src, dst) in enumerate(((w_in_ref, w_in), (w_down_ref, w_down)))
        ]

    @pl.when(step == 0)
    def _():
        greet(
            [rows.device(i, b, c, s) for _, i in rows.along_a()]
            + [rows.device(a, b2, c, s2) for _, b2, s2, _ in rows.plane()]
            + [rows.device(a, b, 1 - c, s)]
            + lay.group_peers()
            + lay.weight_peers()
        )
        A, Q = rows.A, 2 * rows.S
        sl = s if rows.S > 1 else 0
        third = members // 3
        local = pltpu.make_async_copy(own_ref, full.at[a, b, c, sl], ls.at[0])
        local.start()
        copies = [
            remote(own_ref, full.at[a, b, c, sl], ps.at[i], pr.at[i], rows.device(a2, b, c, s))
            for i, a2 in rows.along_a()
        ]
        for copy in copies:
            copy.start()
        for i in range(images):
            cot[i] = pad_rows(cot_ref[i].astype(f32), height).astype(bf16)
        build_c(0, third)
        local.wait()
        for copy in copies:
            copy.wait()
        copies = [
            remote(
                full.at[:, b, c, sl], full.at[:, b, c, sl], ps.at[A + i], pr.at[A + i], rows.device(a, b2, c, s2)
            )
            for i, b2, s2, _ in rows.plane()
        ]
        for copy in copies:
            copy.start()
        build_c(third, members)
        for copy in copies:
            copy.wait()
        last = remote(
            full.at[:, :, c], full.at[:, :, c], ps.at[A + Q], pr.at[A + Q], rows.device(a, b, 1 - c, s)
        )
        last.start()
        for d in range(1, S):
            for copy in weight_copies(d):
                copy.start()

        @pl.when(delta == 0)
        def _():
            for copy in weight_local():
                copy.start()

        @pl.when(delta != 0)
        def _():
            for copy in weight_copies(0):
                copy.start()

        def send(k, carry):
            c_copy(k).start()
            return carry

        lax.fori_loop(1, members, send, 0)
        c_recv[me] = c_send[me]
        last.wait()
        pack_ref[...] = full[...].reshape(pack_ref.shape)
        tail = pack_ref[:, 4 * width :].astype(f32).T
        gains_ref[...] = tail[GAIN_LANE : GAIN_LANE + 8, :]

    inputs = pad_rows(tok_ref[0].astype(f32), height)
    hat, _ = norm_rows(inputs)
    normed = (hat * gains_ref[0:1, :]).astype(bf16)
    qkv = dot(normed, pack_ref[:, 0 : 3 * width]).astype(bf16)
    qkv_ref[0] = qkv
    att, lse = attend(HEADS, qkv, mask_ref[0] > 0, width)
    att_ref[0] = att
    lse_ref[0] = lse
    residual = inputs + dot(att, pack_ref[:, 3 * width : 4 * width])
    res_ref[0] = residual
    hat, _ = norm_rows(residual)
    routed_now = (hat * gains_ref[1:2, :]).astype(bf16)
    routed_ref[0] = routed_now
    routed[step] = routed_now
    probs_ref[0] = router_softmax(dot(routed_now, pack_ref[:, 4 * width :]), experts)

    @pl.when(step == steps - 1)
    def _():
        def dispatch(k, carry):
            pick_rows(jnp.bitwise_xor(me, k), routed, x_send)

            @pl.when(k > 0)
            def _():
                x_copy(k).start()

            return carry

        lax.fori_loop(0, members, dispatch, 0)
        x_recv[me] = x_send[me]
        gwi[...] = jnp.zeros_like(gwi)
        gwd[...] = jnp.zeros_like(gwd)

        for p in range(S):
            for copy_in in range(2):
                span = pl.ds(p * part_rows, part_rows)
                dst = (w_in, w_down)[copy_in].at[span]
                src = (w_in_ref, w_down_ref)[copy_in].at[0]

                @pl.when((delta == 0) & (s == p))
                def _():
                    pltpu.make_async_copy(src, dst, wr.at[2 * p + copy_in]).wait()

                @pl.when((delta != 0) | (s != p))
                def _():
                    remote(src, dst, ws.at[0], wr.at[2 * p + copy_in], (0, 0)).wait_recv()

        mine = lay.expert_of(g, me)
        hidden = w_in.shape[1]
        chunk = min(512, hidden)

        def work(j, carry):
            ks = (2 * j, 2 * j + 1)
            ms = [jnp.bitwise_xor(me, k) for k in ks]

            @pl.when(j > 0)
            def _():
                x_copy(ks[0]).wait()
                c_copy(ks[0]).wait()

            x_copy(ks[1]).wait()
            c_copy(ks[1]).wait()
            x = jnp.concatenate([x_recv[m] for m in ms], axis=0)
            cf = jnp.concatenate([c_recv[m] for m in ms], axis=0).astype(f32)
            probs = router_softmax(dot(x, pack_ref[:, 4 * width :]), experts)
            lane = lax.broadcasted_iota(jnp.int32, probs.shape, 1)
            gate = jnp.sum(jnp.where(lane == mine, probs, 0.0), axis=1, keepdims=True)
            dy = (gate * cf).astype(bf16)
            y, gx = None, None
            for f in range(0, hidden, chunk):
                span = slice(f, f + chunk)
                value, slope = gelu_parts(dot(x, w_in[:, span]))
                act = value.astype(bf16)
                inner_grad = (dot(dy, w_down[:, span]) * slope).astype(bf16)
                y_part, gx_part = dot(act, w_down[:, span], NT), dot(inner_grad, w_in[:, span], NT)
                y = y_part if y is None else y + y_part
                gx = gx_part if gx is None else gx + gx_part
                gwd[:, span] += dot(dy, act, TN)
                gwi[:, span] += dot(x, inner_grad, TN)
            zy = (gate * y).astype(bf16)
            gxb = gx.astype(bf16)
            gate_grad = jnp.broadcast_to(jnp.sum(y * cf, axis=1, keepdims=True), (2 * cap, LANES)).T
            for q in range(2):
                c_send[ms[q]] = gxb[q * cap : (q + 1) * cap]
                x_send[ms[q]] = zy[q * cap : (q + 1) * cap]
                gate_send[ms[q]] = gate_grad[0:8, q * cap : (q + 1) * cap]

            @pl.when(j > 0)
            def _():
                gx_copy(ks[0]).start()
                gate_copy(ks[0]).start()

            gx_copy(ks[1]).start()
            gate_copy(ks[1]).start()
            zy_copy(ks[0]).start()
            zy_copy(ks[1]).start()
            return carry

        lax.fori_loop(0, members // 2, work, 0)
        keeps = [
            pltpu.make_async_copy(c_send.at[me], gx_ref.at[me], ls.at[0]),
            pltpu.make_async_copy(gate_send.at[me], gate_ref.at[me], ls.at[1]),
        ]
        for keep in keeps:
            keep.start()
        gwi_ref[...] = gwi[...].astype(bf16)
        gwd_ref[...] = gwd[...].astype(bf16)
        for keep in keeps:
            keep.wait()
        zy_copy(0).wait()
        for d in range(1, S):
            for copy in weight_copies(d):
                copy.wait_send()

        @pl.when(delta != 0)
        def _():
            for copy in weight_copies(0):
                copy.wait_send()

        def finish(k, carry):
            gx_copy(k).wait()
            gate_copy(k).wait()
            zy_copy(k).wait()
            return carry

        lax.fori_loop(1, members, finish, 0)


def front(lay, rows, experts, cap, own, tokens, mask, cotangent, codes, w_in, w_down):
    S, M = lay.S, lay.N
    images, positions, width = tokens.shape
    height = mask.shape[2]
    hidden = w_in.shape[-1]
    blocks = (M, cap, width)
    full = (rows.A, 2, 2, rows.S) + own.shape
    total = rows.A * 4 * rows.S * own.shape[0]
    dma = lambda n: pltpu.SemaphoreType.DMA((n,))
    count = rows.A + 2 * rows.S + 1
    return pl.pallas_call(
        functools.partial(front_kernel, lay, rows, experts),
        grid=(images,),
        out_shape=(
            Shape((total, own.shape[1]), bf16),
            Shape((8, width), f32),
            Shape((images, height, 3 * width), bf16),
            Shape((images, height, width), bf16),
            Shape((images, height, width), f32),
            Shape((images, height, HEADS), f32),
            Shape((images, height, width), bf16),
            Shape((images, height, LANES), f32),
            Shape(blocks, bf16),
            Shape(blocks, bf16),
            Shape((M, 8, cap), f32),
            Shape((width, hidden), bf16),
            Shape((width, hidden), bf16),
        ),
        in_specs=[
            fixed(*own.shape),
            per_image(positions, width),
            per_image(1, height),
            fixed(*cotangent.shape),
            fixed(*codes.shape),
            anywhere(),
            anywhere(),
        ],
        out_specs=(
            fixed(total, own.shape[1]),
            fixed(8, width),
            per_image(height, 3 * width),
            per_image(height, width),
            per_image(height, width),
            per_image(height, HEADS),
            per_image(height, width),
            per_image(height, LANES),
            anywhere(),
            anywhere(),
            anywhere(),
            fixed(width, hidden),
            fixed(width, hidden),
        ),
        scratch_shapes=[
            pltpu.VMEM(full, bf16),
            pltpu.VMEM((images, height, width), bf16),
            pltpu.VMEM((images, height, width), bf16),
            pltpu.VMEM((width, hidden), bf16),
            pltpu.VMEM((width, hidden), bf16),
            *[pltpu.VMEM(blocks, bf16)] * 4,
            pltpu.VMEM((M, 8, cap), f32),
            pltpu.VMEM((width, hidden), f32),
            pltpu.VMEM((width, hidden), f32),
            dma(count), dma(count), dma(2 * S), dma(2 * S),
            *[dma(M)] * 9,
            dma(2),
        ],
        compiler_params=pltpu.CompilerParams(
            collective_id=0, has_side_effects=True, vmem_limit_bytes=VMEM_LIMIT, dimension_semantics=("arbitrary",)
        ),
    )(own, tokens, mask, cotangent, codes, w_in, w_down)


def back_kernel(
    lay, rows,
    tok_ref, mask_ref, cot_ref, code_ref, qkv_ref, att_ref, res_ref, lse_ref, routed_ref, probs_ref,
    pack_ref, gains_ref, gx_ref, gate_ref, zy_ref, gwi_ref, gwd_ref,
    gtok_ref, mixed_ref, own_ref, gwi_parts, gwd_parts,
    gqkv, gout, grest, table, ggain, residuals, codes, zy, part, recv1, sum1, recv2, sum2, recv3,
    ps, pr, zs, zr, ws, wr, ls,
):
    step = pl.program_id(0)
    images = pl.num_programs(0)
    a, b, c, s = rows.here()
    _, _, g, l = lay.here()
    S, L = lay.S, lay.L
    me = l * S + s
    delta = lax.rem(s + l, S)
    members, _, cap = gate_ref.shape
    slots = members * cap
    height, width = att_ref.shape[1], att_ref.shape[2]
    positions = gtok_ref.shape[1]
    head = width // HEADS
    part_rows = gwi_ref.shape[0] // S

    def remote(src, dst, send, recv, device):
        return pltpu.make_async_remote_copy(src, dst, send, recv, device_id=device, device_id_type=MESH)

    def zy_copy(k):
        m = jnp.bitwise_xor(me, k)
        return remote(zy_ref.at[m], zy.at[me], zs.at[k], zr.at[k], lay.member_device(g, m))

    owner = lax.rem(g + delta, S)

    def weight_pairs(p):
        span = pl.ds(p * part_rows, part_rows)
        return ((gwi_ref.at[span], gwi_parts.at[g]), (gwd_ref.at[span], gwd_parts.at[g]))

    def weight_copies(p):
        return [
            remote(src, dst, ws.at[2 * p + i], wr.at[2 * g + i], (owner * L + l, p))
            for i, (src, dst) in enumerate(weight_pairs(p))
        ]

    def weight_local(p):
        return [
            pltpu.make_async_copy(src, dst, ws.at[2 * p + i]) for i, (src, dst) in enumerate(weight_pairs(p))
        ]

    def for_parts(remote_do, local_do):
        for p in range(S):
            @pl.when((delta == 0) & (s == p))
            def _():
                for copy in weight_local(p):
                    local_do(copy)

            @pl.when((delta != 0) | (s != p))
            def _():
                for copy in weight_copies(p):
                    remote_do(copy)

    zy_keep = pltpu.make_async_copy(zy_ref.at[me], zy.at[me], ls.at[0])

    @pl.when(step == 0)
    def _():
        greet(
            [rows.device(i, b, c, s) for _, i in rows.along_a()]
            + [rows.device(a, b2, c, s2) for _, b2, s2, _ in rows.plane()]
            + [rows.device(a, b, 1 - c, s)]
            + lay.group_peers()
            + lay.weight_peers()
        )
        for_parts(lambda copy: copy.start(), lambda copy: copy.start())

        def send(k, carry):
            zy_copy(k).start()
            return carry

        lax.fori_loop(1, members, send, 0)
        zy_keep.start()
        for ref in (gqkv, gout, grest, ggain):
            ref[...] = jnp.zeros_like(ref)
        for m in range(members):
            values = gate_ref[m][0:1, :]
            high = values.astype(bf16).astype(f32)
            sub = lax.broadcasted_iota(jnp.int32, (LANES, cap), 0)
            here = sub == lay.expert_of(g, jnp.int32(m))
            span = slice(m * cap, (m + 1) * cap)
            table[0:LANES, span] = jnp.where(here, high, 0.0).astype(bf16)
            table[LANES : 2 * LANES, span] = jnp.where(here, values - high, 0.0).astype(bf16)

    def pick_slots(code):
        slot = lax.broadcasted_iota(jnp.int32, (height, slots), 1)
        return jnp.where((code[:, 0:1] == slot) | (code[:, 1:2] == slot), 1.0, 0.0).astype(bf16)

    code = code_ref[0]
    codes[step] = code
    residuals[step] = res_ref[0]
    pick = pick_slots(code)
    grad_routed = dot(pick, gx_ref[...].reshape(slots, width))
    both = dot(pick, table[...], NT)
    grad_probs = both[:, :LANES] + both[:, LANES:]
    probs = probs_ref[0]
    grad_logits = probs * (grad_probs - jnp.sum(grad_probs * probs, axis=1, keepdims=True))
    logit_high = grad_logits.astype(bf16)
    logit_low = (grad_logits - logit_high.astype(f32)).astype(bf16)
    router = pack_ref[:, 4 * width :]
    grad_router = dot(routed_ref[0], jnp.concatenate([logit_high, logit_low], axis=1), TN)
    grest[...] += grad_router[:, :LANES] + grad_router[:, LANES:]
    grad_routed += dot(logit_high, router, NT) + dot(logit_low, router, NT)
    hat_two, inverse_two = norm_rows(res_ref[0])
    ggain[1:2, :] += jnp.sum(grad_routed * hat_two, axis=0, keepdims=True)
    grad_residual = pad_rows(cot_ref[0].astype(f32), height) + norm_back(
        grad_routed * gains_ref[1:2, :], hat_two, inverse_two
    )
    grad_att = grad_residual.astype(bf16)
    gout[...] += dot(att_ref[0], grad_att, TN)
    grad_attended = dot(grad_att, pack_ref[:, 3 * width : 4 * width], NT).astype(bf16)
    keep = mask_ref[0] > 0
    qkv, lse = qkv_ref[0], lse_ref[0]
    scale = head**-0.5
    grad_q, grad_k, grad_v = [], [], []
    for h in range(HEADS):
        q = qkv[:, h * head : (h + 1) * head]
        k = qkv[:, width + h * head : width + (h + 1) * head]
        v = qkv[:, 2 * width + h * head : 2 * width + (h + 1) * head]
        ga = grad_attended[:, h * head : (h + 1) * head]
        scores = jnp.where(keep, dot(q, k, NT) * scale, NEGATIVE)
        weights = jnp.exp(scores - lse[:, h : h + 1])
        grad_v.append(dot(weights.astype(bf16), ga, TN).astype(bf16))
        grad_weights = dot(ga, v, NT)
        row = jnp.sum(weights * grad_weights, axis=1, keepdims=True)
        grad_scores = (weights * (grad_weights - row)).astype(bf16)
        grad_q.append((dot(grad_scores, k) * scale).astype(bf16))
        grad_k.append((dot(grad_scores, q, TN) * scale).astype(bf16))
    grad_qkv = jnp.concatenate(grad_q + grad_k + grad_v, axis=1)
    hat_one, inverse_one = norm_rows(pad_rows(tok_ref[0].astype(f32), height))
    normed = (hat_one * gains_ref[0:1, :]).astype(bf16)
    gqkv[...] += dot(normed, grad_qkv, TN)
    grad_normed = dot(grad_qkv, pack_ref[:, 0 : 3 * width], NT)
    ggain[0:1, :] += jnp.sum(grad_normed * hat_one, axis=0, keepdims=True)
    grad_inputs = grad_residual + norm_back(grad_normed * gains_ref[0:1, :], hat_one, inverse_one)
    gtok_ref[0] = grad_inputs[:positions]

    @pl.when(step == images - 1)
    def _():
        A, Q = rows.A, 2 * rows.S
        zeros = jnp.zeros((GAIN_LANE, width), f32)
        tail = jnp.concatenate([zeros, ggain[...], zeros[: GAIN_LANE - 8]], axis=0)
        grest[...] += tail.T
        shape = part.shape[:5]
        part[..., 0 : 3 * width] = gqkv[...].astype(bf16).reshape(shape + (3 * width,))
        part[..., 3 * width : 4 * width] = gout[...].astype(bf16).reshape(shape + (width,))
        part[..., 4 * width :] = grest[...].astype(bf16).reshape(shape + (LANES,))
        first = remote(part.at[:, :, 1 - c], recv1, ps.at[0], pr.at[0], rows.device(a, b, 1 - c, s))
        first.start()

        def wait_zy(k, carry):
            zy_copy(k).wait()
            return carry

        lax.fori_loop(1, members, wait_zy, 0)
        zy_keep.wait()

        def mix(first_image, last_image):
            def one(i, carry):
                mixed = residuals[i] + dot(pick_slots(codes[i]), zy[...].reshape(slots, width))
                mixed_ref[i] = mixed[:positions].astype(bf16)
                return carry

            lax.fori_loop(first_image, last_image, one, 0)

        count = residuals.shape[0]
        mix(0, count // 4)
        first.wait()
        sum1[...] = (part[:, :, c].astype(f32) + recv1[...].astype(f32)).astype(bf16)
        copies = [
            remote(sum1.at[:, b2, sl2], recv2.at[i - 1], ps.at[i], pr.at[i], rows.device(a, b2, c, s2))
            for i, b2, s2, sl2 in rows.plane()
        ]
        for copy in copies:
            copy.start()
        mix(count // 4, count * 3 // 4)
        for copy in copies:
            copy.wait()
        sl = s if rows.S > 1 else 0
        total = sum1[:, b, sl].astype(f32)
        for i in range(Q - 1):
            total += recv2[i].astype(f32)
        sum2[...] = total.astype(bf16)
        copies = [
            remote(sum2.at[a2], recv3.at[i - 1], ps.at[Q + i], pr.at[Q + i], rows.device(a2, b, c, s))
            for i, a2 in rows.along_a()
        ]
        for copy in copies:
            copy.start()
        mix(count * 3 // 4, count)
        for copy in copies:
            copy.wait()
        final = sum2[a].astype(f32)
        for i in range(A - 1):
            final += recv3[i].astype(f32)
        own_ref[...] = final

        for_parts(lambda copy: copy.wait_send(), lambda copy: copy.wait())
        for q in range(S):
            @pl.when((delta != 0) | (g != q))
            def _():
                for i, (src, dst) in enumerate(((gwi_ref, gwi_parts), (gwd_ref, gwd_parts))):
                    span = pl.ds(0, part_rows)
                    remote(src.at[span], dst.at[q], ws.at[i], wr.at[2 * q + i], (0, 0)).wait_recv()


def back(
    lay, rows, own_height, tokens, mask, cotangent, code, qkv, att, res, lse, routed, probs, pack, gains, gx, gate,
    zy, gwi, gwd,
):
    images, positions, width = tokens.shape
    height = att.shape[1]
    M, _, cap = gate.shape
    slots = M * cap
    A, S = rows.A, rows.S
    G = lay.S
    hidden = gwi.shape[1]
    part_rows = gwi.shape[0] // G
    columns = pack.shape[1]
    dma = lambda n: pltpu.SemaphoreType.DMA((n,))
    count = A + 2 * S + 1
    return pl.pallas_call(
        functools.partial(back_kernel, lay, rows),
        grid=(images,),
        out_shape=(
            Shape((images, positions, width), f32),
            Shape((images, positions, width), bf16),
            Shape((own_height, columns), f32),
            Shape((G, part_rows, hidden), bf16),
            Shape((G, part_rows, hidden), bf16),
        ),
        in_specs=[
            per_image(positions, width),
            per_image(1, height),
            per_image(positions, width),
            per_image(height, 2),
            per_image(height, 3 * width),
            per_image(height, width),
            per_image(height, width),
            per_image(height, HEADS),
            per_image(height, width),
            per_image(height, LANES),
            fixed(*pack.shape),
            fixed(*gains.shape),
            fixed(*gx.shape),
            fixed(*gate.shape),
            anywhere(),
            anywhere(),
            anywhere(),
        ],
        out_specs=(
            per_image(positions, width),
            fixed(images, positions, width),
            fixed(own_height, columns),
            anywhere(),
            anywhere(),
        ),
        scratch_shapes=[
            pltpu.VMEM((width, 3 * width), f32),
            pltpu.VMEM((width, width), f32),
            pltpu.VMEM((width, LANES), f32),
            pltpu.VMEM((2 * LANES, slots), bf16),
            pltpu.VMEM((8, width), f32),
            pltpu.VMEM((images, height, width), f32),
            pltpu.VMEM((images, height, 2), jnp.int32),
            pltpu.VMEM((M, cap, width), bf16),
            pltpu.VMEM((A, 2, 2, S, own_height, columns), bf16),
            pltpu.VMEM((A, 2, S, own_height, columns), bf16),
            pltpu.VMEM((A, 2, S, own_height, columns), bf16),
            pltpu.VMEM((2 * S - 1, A, own_height, columns), bf16),
            pltpu.VMEM((A, own_height, columns), bf16),
            pltpu.VMEM((A - 1, own_height, columns), bf16),
            dma(count), dma(count), dma(M), dma(M), dma(2 * G), dma(2 * G), dma(1),
        ],
        compiler_params=pltpu.CompilerParams(
            collective_id=1, has_side_effects=True, vmem_limit_bytes=VMEM_LIMIT, dimension_semantics=("arbitrary",)
        ),
    )(tokens, mask, cotangent, code, qkv, att, res, lse, routed, probs, pack, gains, gx, gate, zy, gwi, gwd)


def body(
    lay, tokens, w_qkv, w_attn_out, w_router, gain_attn, gain_moe, w_expert_in, w_expert_down, key_mask,
    expert_choice, slot_index, cotangent,
):
    images, positions, width = tokens.shape
    N, S, L = lay.N, lay.S, lay.L
    experts = w_router.shape[1]
    height = -(-positions // 16) * 16
    token_rows = images * positions
    capacity = ((token_rows * 10 + 4 * experts - 1) // (4 * experts) + 7) // 8 * 8
    dp, s, g, l = lay.here()

    lane = jnp.arange(LANES, dtype=jnp.int32)[None, :]
    rest = jnp.pad(w_router, ((0, 0), (0, LANES - experts)))
    rest = jnp.where(lane == GAIN_LANE, gain_attn[:, None], jnp.where(lane == GAIN_LANE + 1, gain_moe[:, None], rest))
    own = jnp.concatenate([w_qkv, w_attn_out, rest], axis=1)
    few = w_qkv.shape[0] % 16 != 0
    if few:
        own = lax.all_gather(own, "seq", axis=0, tiled=True)
    rows = Rows(N, 1 if few else S)

    mask = lax.dynamic_slice_in_dim(key_mask, s * images, images, axis=0)
    mask = jnp.pad(mask, ((0, 0), (0, height - positions)))[:, None, :]
    group, local = expert_choice // L, lax.rem(expert_choice, L)
    member = local * S + lax.rem(group - g - local + (L + 1) * S, S)
    code = jnp.where(slot_index >= 0, member * capacity + slot_index, -1)
    code = jnp.pad(code, ((0, 0), (0, height - positions), (0, 0)), constant_values=-1)
    code_rows = code.reshape(images * height, 2).T

    pack, gains, qkv, att, res, lse, routed, probs, gx, zy, gate, gwi, gwd = front(
        lay, rows, experts, capacity, own, tokens, mask, cotangent, code_rows, w_expert_in, w_expert_down
    )
    gtok, mixed, sums, gwi, gwd = back(
        lay, rows, own.shape[0], tokens, mask, cotangent, code, qkv, att, res, lse, routed, probs, pack, gains, gx,
        gate, zy, gwi, gwd,
    )
    if few:
        sums = lax.psum_scatter(sums, "seq", scatter_dimension=0, tiled=True)
    rest = sums[:, 4 * width :]
    return (
        mixed,
        gtok,
        sums[:, : 3 * width],
        sums[:, 3 * width : 4 * width],
        rest[:, :experts],
        rest[:, GAIN_LANE],
        rest[:, GAIN_LANE + 1],
        jnp.sum(gwi.astype(f32), axis=0, keepdims=True),
        jnp.sum(gwd.astype(f32), axis=0, keepdims=True),
    )


def solution(mesh):
    lay = Layout(mesh.shape["dp"], mesh.shape["seq"])
    return jax.shard_map(
        functools.partial(body, lay),
        mesh=mesh,
        in_specs=(
            P(("dp", "seq"), None, None),
            P(("dp", "seq"), None),
            P(("dp", "seq"), None),
            P(("dp", "seq"), None),
            P(("dp", "seq")),
            P(("dp", "seq")),
            P("dp", "seq", None),
            P("dp", "seq", None),
            P("dp", None),
            P(("dp", "seq"), None, None),
            P(("dp", "seq"), None, None),
            P(("dp", "seq"), None, None),
        ),
        out_specs=(
            P(("dp", "seq"), None, None),
            P(("dp", "seq"), None, None),
            P(("dp", "seq"), None),
            P(("dp", "seq"), None),
            P(("dp", "seq"), None),
            P(("dp", "seq")),
            P(("dp", "seq")),
            P("dp", "seq", None),
            P("dp", "seq", None),
        ),
        check_vma=False,
    )
```

time: 610 us -> 420 us (0.69); the launches traced: 599 us -> 419 us
  Pallas kernels: 478 us -> 394 us
  waiting for transfers between devices: 56.8 us -> 0 us
  starting transfers between devices: 32.4 us -> 0 us
    pallas_call x6 -> x2, Pallas kernels: 478 us -> 394 us  [the longest x1 245 us: front(): pl.pallas_call(functools.partial(front_kernel, lay, rows, experts), grid=...]
    ppermute x8 -> x0, waiting for transfers between devices: 56.8 us -> none  [the longest x4 56.8 us: body(): part = lax.ppermute(partial[j:j + 1], ('dp', 'seq'), back).astype(f32)]
    ppermute x8 -> x0, starting transfers between devices: 32.4 us -> none  [the longest x4 11.8 us: body(): part = lax.ppermute(partial[j:j + 1], ('dp', 'seq'), back).astype(f32)]
    add x2 -> x0, other arithmetic: 6.14 us -> none  [body(): total = part if total is None else total + part]
  transfers between devices with their start and end apart: 8 -> 0, of which waited for: 2 -> 0; matrix products, arithmetic and copies ran while one was open for 3% -> 0% of each run, Pallas kernels for 22% -> 0%
where the time goes in v2:
time: 420 us; the launch traced here: 419 us
  Pallas kernels  394 us (94%)
  local copies, waits for them, and re-layouts  14.3 us (3%)
  other arithmetic  10 us (2%)
    pallas_call x1, Pallas kernels, front(): pl.pallas_call(functools.partial(front_kernel, lay, rows, experts), grid=...  245 us
    pallas_call x1, Pallas kernels, back(): pl.pallas_call(functools.partial(back_kernel, lay, rows), grid=(images,),...  150 us

profile of v2, /device:TPU:0, one launch (start us, length us, event | category | flops | bytes accessed | tf_op | source)
XLA Modules:
  0.0 419.3 jit_solution(12070153674680890049)
XLA Ops:
  0.7 0.8 select_select_fusion
  1.5 0.6 broadcast_in_dim.40.mask_ref
  2.1 0.7 broadcast_compare_fusion
  2.8 0.7 broadcast_compare_fusion.1
  3.6 1.5 pad_maximum_fusion.own_ref
  5.0 0.4 copy.63
  5.4 0.4 copy.56
  5.8 1.0 copy.53
  6.9 0.7 negate_select_fusion.3
  7.6 0.3 copy.57
  8.0 0.3 copy.61
  8.3 0.3 copy.64
  8.8 0.9 copy.65
  9.7 244.6 %shard_map.187 = (bf16[512,2176]{1,0:T(8,128)(2,1)}, f32[8,512]{1,0:T(8,128)}, bf16[8,208,1536]{2,1,0:T(8,128)(2,1)}, bf16[8,208,512]{2,1,0:T(8,128)(2,1)}, f32[...) custom-call(bf16[16,2176]{1,0:T(8,128)(2,1)} %pad_maximum_fusion.own, ...), custom_call_target="tpu_custom_call" | custom-call | tf_op jit(solution)/shard_map/pallas_call | solution.py:425
  254.4 149.5 %shard_map.188 = (f32[8,200,512]{2,1,0:T(8,128)}, bf16[8,200,512]{2,1,0:T(8,128)(2,1)}, f32[16,2176]{1,0:T(8,128)}, bf16[2,256,2048]{2,1,0:T(8,128)(2,1)}, bf16[2,256,2048]{2,1,0:T(8,128)(2,1)}) custom-call(bf16[8,200,512]{2,1,0:T(8,128)(2,1)} %tok_ref.3, s32[8,1,208]{2,1,0:T(1,128)} %broadcast_in_dim.40.mask_ref, bf16[8,200,512]{2,1,0:T(8,128)(2,1)} %cot_ref.3, ...), custom_call_target="tpu_custom_call" | custom-call | tf_op jit(solution)/shard_map/pallas_call | solution.py:712
  403.9 1.5 slice_reduce_fusion
  405.4 1.3 slice.21
  406.7 1.4 slice.20
  408.0 1.5 slice.19
  409.6 3.7 convert_reduce_fusion.1
  413.3 1.8 convert_reduce_fusion
  415.0 1.2 copy.73
  416.2 1.3 copy-done.2
  417.6 1.7 copy.74
  (17 shorter events, 0.2 us)
Async XLA Ops:
  0.6 0.8 copy-start
  6.9 1.4 copy-start.5
  8.8 245.6 %copy-start.1 = (s32[8,208,2]{2,1,0:T(8,128)}, s32[8,208,2]{2,1,0:T(8,128)S(1)}, u32[]{:S(2)}) copy-start(s32[8,208,2]{2,1,0:T(8,128)S(1)} %pad.13.code_ref) | copy-start | bytes 39940
  409.6 3.7 copy-start.3
  413.3 1.8 copy-start.4
  415.0 2.5 copy-start.2

commit v3 on v2

--- a/solution.py
+++ b/solution.py
@@ -96,6 +96,26 @@
         count = self.S * self.S
         places = [lax.rem(g * self.S + s + i, count) for i in range(1, count)]
         return [(q // self.S * self.L + l, lax.rem(q, self.S)) for q in places]
+
+    def order(self):
+        bits = [1 << i for i in range(self.N.bit_length() - 1) if 1 << i != self.S]
+        left, loads, picked = list(range(1, self.N)), [0] * len(bits), []
+
+        def after(k):
+            return [load + (k & bit > 0) for load, bit in zip(loads, bits)]
+
+        while left:
+            k = min(left, key=lambda k: (max(after(k)) - min(after(k)), -sum(after(k)), k))
+            left.remove(k)
+            picked.append(k)
+            loads = after(k)
+        return picked
+
+    def nth(self, i):
+        k = jnp.int32(0)
+        for n, value in enumerate(self.order()):
+            k = jnp.where(i == n + 1, value, k)
+        return k
 
     def expert_of(self, g, m):
         l, s = m // self.S, lax.rem(m, self.S)
@@ -152,10 +172,10 @@
 
 def front_kernel(
     lay, rows, experts,
-    own_ref, tok_ref, mask_ref, cot_ref, code_ref, w_in_ref, w_down_ref,
+    own_refs, tok_ref, mask_ref, cot_ref, code_ref, w_in_ref, w_down_ref,
     pack_ref, gains_ref, qkv_ref, att_ref, res_ref, lse_ref, routed_ref, probs_ref,
     gx_ref, zy_ref, gate_ref, gwi_ref, gwd_ref,
-    full, routed, cot, w_in, w_down, x_send, c_send, x_recv, c_recv, gate_send, gwi, gwd,
+    own, full, routed, cot, w_in, w_down, x_send, c_send, x_recv, c_recv, gate_send, gwi, gwd,
     ps, pr, ws, wr, xs, xr, cs, cr, gs, gr, ts, tr, zs, ls,
 ):
     step = pl.program_id(0)
@@ -168,6 +188,7 @@
     me = l * S + s
     delta = lax.rem(s + l, S)
     part_rows = w_in.shape[0] // S
+    piece_rows = max(part_rows // 8, 16)
 
     def remote(src, dst, send, recv, device):
         return pltpu.make_async_remote_copy(src, dst, send, recv, device_id=device, device_id_type=MESH)
@@ -198,19 +219,23 @@
         target[m] = dot(pick, values[...].reshape(images * height, width)).astype(bf16)
 
     def build_c(first, last):
-        def build(k, carry):
-            pick_rows(jnp.bitwise_xor(me, k), cot, c_send)
+        def build(i, carry):
+            pick_rows(jnp.bitwise_xor(me, lay.nth(i + 1)), cot, c_send)
             return carry
 
         lax.fori_loop(first, last, build, 0)
 
-    def weight_copies(d):
+    def weight_copies(d, first=0, count=part_rows):
         device = (lax.rem(g - d + S, S) * L + l, lax.rem(d - l + L * S, S))
-        mine = pl.ds(pl.multiple_of(s * part_rows, part_rows), part_rows)
+        there = pl.ds(pl.multiple_of(s * part_rows + first, 16), count)
         return [
-            remote(src.at[0], dst.at[mine], ws.at[2 * d + i], wr.at[2 * s + i], device)
+            remote(src.at[0, pl.ds(first, count)], dst.at[there], ws.at[2 * d + i], wr.at[2 * s + i], device)
             for i, (src, dst) in enumerate(((w_in_ref, w_in), (w_down_ref, w_down)))
         ]
+
+    def weight_pieces(d, q):
+        for copy in weight_copies(d, q * piece_rows, piece_rows):
+            copy.start()
 
     def weight_local():
         mine = pl.ds(pl.multiple_of(s * part_rows, part_rows), part_rows)
@@ -230,11 +255,31 @@
         )
         A, Q = rows.A, 2 * rows.S
         sl = s if rows.S > 1 else 0
+        first = 0
+        for ref in own_refs:
+            own[:, first : first + ref.shape[1]] = ref[...]
+            first += ref.shape[1]
         third = members // 3
-        local = pltpu.make_async_copy(own_ref, full.at[a, b, c, sl], ls.at[0])
+        order = lay.order()
+        pieces = part_rows // piece_rows
+        todo = [(q, d) for q in range(pieces) for d in (*range(1, S), 0)]
+
+        def send(first, last):
+            for n in range(first, last):
+                c_copy(order[n]).start()
+                for q, d in todo[n * len(todo) // len(order) : (n + 1) * len(todo) // len(order)]:
+                    if d:
+                        weight_pieces(d, q)
+                    else:
+
+                        @pl.when(delta != 0)
+                        def _():
+                            weight_pieces(0, q)
+
+        local = pltpu.make_async_copy(own, full.at[a, b, c, sl], ls.at[0])
         local.start()
         copies = [
-            remote(own_ref, full.at[a, b, c, sl], ps.at[i], pr.at[i], rows.device(a2, b, c, s))
+            remote(own, full.at[a, b, c, sl], ps.at[i], pr.at[i], rows.device(a2, b, c, s))
             for i, a2 in rows.along_a()
         ]
         for copy in copies:
@@ -260,25 +305,13 @@
             full.at[:, :, c], full.at[:, :, c], ps.at[A + Q], pr.at[A + Q], rows.device(a, b, 1 - c, s)
         )
         last.start()
-        for d in range(1, S):
-            for copy in weight_copies(d):
-                copy.start()
 
         @pl.when(delta == 0)
         def _():
             for copy in weight_local():
                 copy.start()
 
-        @pl.when(delta != 0)
-        def _():
-            for copy in weight_copies(0):
-                copy.start()
-
-        def send(k, carry):
-            c_copy(k).start()
-            return carry
-
-        lax.fori_loop(1, members, send, 0)
+        send(0, members - 1)
         c_recv[me] = c_send[me]
         last.wait()
         pack_ref[...] = full[...].reshape(pack_ref.shape)
@@ -303,16 +336,14 @@
 
     @pl.when(step == steps - 1)
     def _():
-        def dispatch(k, carry):
+        def dispatch(i, carry):
+            k = lay.nth(i)
             pick_rows(jnp.bitwise_xor(me, k), routed, x_send)
-
-            @pl.when(k > 0)
-            def _():
-                x_copy(k).start()
-
+            x_copy(k).start()
             return carry
 
-        lax.fori_loop(0, members, dispatch, 0)
+        lax.fori_loop(1, members, dispatch, 0)
+        pick_rows(me, routed, x_send)
         x_recv[me] = x_send[me]
         gwi[...] = jnp.zeros_like(gwi)
         gwd[...] = jnp.zeros_like(gwd)
@@ -336,7 +367,7 @@
         chunk = min(512, hidden)
 
         def work(j, carry):
-            ks = (2 * j, 2 * j + 1)
+            ks = (lay.nth(2 * j), lay.nth(2 * j + 1))
             ms = [jnp.bitwise_xor(me, k) for k in ks]
 
             @pl.when(j > 0)
@@ -418,15 +449,16 @@
     height = mask.shape[2]
     hidden = w_in.shape[-1]
     blocks = (M, cap, width)
-    full = (rows.A, 2, 2, rows.S) + own.shape
-    total = rows.A * 4 * rows.S * own.shape[0]
+    own_shape = (own[0].shape[0], sum(part.shape[1] for part in own))
+    full = (rows.A, 2, 2, rows.S) + own_shape
+    total = rows.A * 4 * rows.S * own_shape[0]
     dma = lambda n: pltpu.SemaphoreType.DMA((n,))
     count = rows.A + 2 * rows.S + 1
     return pl.pallas_call(
         functools.partial(front_kernel, lay, rows, experts),
         grid=(images,),
         out_shape=(
-            Shape((total, own.shape[1]), bf16),
+            Shape((total, own_shape[1]), bf16),
             Shape((8, width), f32),
             Shape((images, height, 3 * width), bf16),
             Shape((images, height, width), bf16),
@@ -441,7 +473,7 @@
             Shape((width, hidden), bf16),
         ),
         in_specs=[
-            fixed(*own.shape),
+            [fixed(*part.shape) for part in own],
             per_image(positions, width),
             per_image(1, height),
             fixed(*cotangent.shape),
@@ -450,7 +482,7 @@
             anywhere(),
         ],
         out_specs=(
-            fixed(total, own.shape[1]),
+            fixed(total, own_shape[1]),
             fixed(8, width),
             per_image(height, 3 * width),
             per_image(height, width),
@@ -465,6 +497,7 @@
             fixed(width, hidden),
         ),
         scratch_shapes=[
+            pltpu.VMEM(own_shape, bf16),
             pltpu.VMEM(full, bf16),
             pltpu.VMEM((images, height, width), bf16),
             pltpu.VMEM((images, height, width), bf16),
@@ -505,6 +538,7 @@
     positions = gtok_ref.shape[1]
     head = width // HEADS
     part_rows = gwi_ref.shape[0] // S
+    piece_rows = max(part_rows // 8, 16)
 
     def remote(src, dst, send, recv, device):
         return pltpu.make_async_remote_copy(src, dst, send, recv, device_id=device, device_id_type=MESH)
@@ -515,14 +549,14 @@
 
     owner = lax.rem(g + delta, S)
 
-    def weight_pairs(p):
-        span = pl.ds(p * part_rows, part_rows)
-        return ((gwi_ref.at[span], gwi_parts.at[g]), (gwd_ref.at[span], gwd_parts.at[g]))
-
-    def weight_copies(p):
+    def weight_pairs(p, first=0, count=part_rows):
+        span, there = pl.ds(p * part_rows + first, count), pl.ds(first, count)
+        return ((gwi_ref.at[span], gwi_parts.at[g, there]), (gwd_ref.at[span], gwd_parts.at[g, there]))
+
+    def weight_copies(p, first=0, count=part_rows):
         return [
             remote(src, dst, ws.at[2 * p + i], wr.at[2 * g + i], (owner * L + l, p))
-            for i, (src, dst) in enumerate(weight_pairs(p))
+            for i, (src, dst) in enumerate(weight_pairs(p, first, count))
         ]
 
     def weight_local(p):
@@ -530,17 +564,11 @@
             pltpu.make_async_copy(src, dst, ws.at[2 * p + i]) for i, (src, dst) in enumerate(weight_pairs(p))
         ]
 
-    def for_parts(remote_do, local_do):
-        for p in range(S):
-            @pl.when((delta == 0) & (s == p))
-            def _():
-                for copy in weight_local(p):
-                    local_do(copy)
-
-            @pl.when((delta != 0) | (s != p))
-            def _():
-                for copy in weight_copies(p):
-                    remote_do(copy)
+    def weight_pieces(p, q):
+        @pl.when((delta != 0) | (s != p))
+        def _():
+            for copy in weight_copies(p, q * piece_rows, piece_rows):
+                copy.start()
 
     zy_keep = pltpu.make_async_copy(zy_ref.at[me], zy.at[me], ls.at[0])
 
@@ -553,35 +581,42 @@
             + lay.group_peers()
             + lay.weight_peers()
         )
-        for_parts(lambda copy: copy.start(), lambda copy: copy.start())
-
-        def send(k, carry):
+        pieces = part_rows // piece_rows
+        todo = [(p, q) for q in range(pieces) for p in range(S)]
+        order = lay.order()
+        for n, k in enumerate(order):
+            for p, q in todo[n * len(todo) // len(order) : (n + 1) * len(todo) // len(order)]:
+                weight_pieces(p, q)
             zy_copy(k).start()
-            return carry
-
-        lax.fori_loop(1, members, send, 0)
         zy_keep.start()
+        for p in range(S):
+
+            @pl.when((delta == 0) & (s == p))
+            def _():
+                for copy in weight_local(p):
+                    copy.start()
+
         for ref in (gqkv, gout, grest, ggain):
             ref[...] = jnp.zeros_like(ref)
         for m in range(members):
-            values = gate_ref[m][0:1, :]
+            values = gate_ref[m].T[:, 0:1]
             high = values.astype(bf16).astype(f32)
-            sub = lax.broadcasted_iota(jnp.int32, (LANES, cap), 0)
-            here = sub == lay.expert_of(g, jnp.int32(m))
+            lane = lax.broadcasted_iota(jnp.int32, (cap, LANES), 1)
+            here = lane == lay.expert_of(g, jnp.int32(m))
             span = slice(m * cap, (m + 1) * cap)
-            table[0:LANES, span] = jnp.where(here, high, 0.0).astype(bf16)
-            table[LANES : 2 * LANES, span] = jnp.where(here, values - high, 0.0).astype(bf16)
+            table[span, 0:LANES] = jnp.where(here, high, 0.0).astype(bf16)
+            table[span, LANES : 2 * LANES] = jnp.where(here, values - high, 0.0).astype(bf16)
 
     def pick_slots(code):
         slot = lax.broadcasted_iota(jnp.int32, (height, slots), 1)
         return jnp.where((code[:, 0:1] == slot) | (code[:, 1:2] == slot), 1.0, 0.0).astype(bf16)
 
-    code = code_ref[0]
-    codes[step] = code
+    wide = jnp.concatenate([code_ref[0].astype(f32), jnp.zeros((6, height), f32)], axis=0)
+    codes[step] = wide.T.astype(jnp.int32)
     residuals[step] = res_ref[0]
-    pick = pick_slots(code)
+    pick = pick_slots(codes[step])
     grad_routed = dot(pick, gx_ref[...].reshape(slots, width))
-    both = dot(pick, table[...], NT)
+    both = dot(pick, table[...])
     grad_probs = both[:, :LANES] + both[:, LANES:]
     probs = probs_ref[0]
     grad_logits = probs * (grad_probs - jnp.sum(grad_probs * probs, axis=1, keepdims=True))
@@ -685,7 +720,18 @@
             final += recv3[i].astype(f32)
         own_ref[...] = final
 
-        for_parts(lambda copy: copy.wait_send(), lambda copy: copy.wait())
+        for p in range(S):
+
+            @pl.when((delta == 0) & (s == p))
+            def _():
+                for copy in weight_local(p):
+                    copy.wait()
+
+            @pl.when((delta != 0) | (s != p))
+            def _():
+                for copy in weight_copies(p):
+                    copy.wait_send()
+
         for q in range(S):
             @pl.when((delta != 0) | (g != q))
             def _():
@@ -723,7 +769,7 @@
             per_image(positions, width),
             per_image(1, height),
             per_image(positions, width),
-            per_image(height, 2),
+            per_image(2, height),
             per_image(height, 3 * width),
             per_image(height, width),
             per_image(height, width),
@@ -749,10 +795,10 @@
             pltpu.VMEM((width, 3 * width), f32),
             pltpu.VMEM((width, width), f32),
             pltpu.VMEM((width, LANES), f32),
-            pltpu.VMEM((2 * LANES, slots), bf16),
+            pltpu.VMEM((slots, 2 * LANES), bf16),
             pltpu.VMEM((8, width), f32),
             pltpu.VMEM((images, height, width), f32),
-            pltpu.VMEM((images, height, 2), jnp.int32),
+            pltpu.VMEM((images, height, 8), jnp.int32),
             pltpu.VMEM((M, cap, width), bf16),
             pltpu.VMEM((A, 2, 2, S, own_height, columns), bf16),
             pltpu.VMEM((A, 2, S, own_height, columns), bf16),
@@ -768,6 +814,62 @@
     )(tokens, mask, cotangent, code, qkv, att, res, lse, routed, probs, pack, gains, gx, gate, zy, gwi, gwd)
 
 
+def finish_kernel(sums_ref, gwi_parts, gwd_parts, qkv_ref, out_ref, router_ref, gain_one, gain_two, gwi_ref, gwd_ref):
+    width = out_ref.shape[1]
+    step = pl.program_id(0)
+
+    @pl.when(step == 0)
+    def _():
+        qkv_ref[...] = sums_ref[:, : 3 * width]
+        out_ref[...] = sums_ref[:, 3 * width : 4 * width]
+        rest = sums_ref[:, 4 * width :]
+        router_ref[...] = rest[:, : router_ref.shape[1]]
+        height = rest.shape[0]
+        tall = pad_rows(rest, max(height, 8)).T
+        gain_one[...] = tall[GAIN_LANE : GAIN_LANE + 1, :height]
+        gain_two[...] = tall[GAIN_LANE + 1 : GAIN_LANE + 2, :height]
+
+    for parts, ref in ((gwi_parts, gwi_ref), (gwd_parts, gwd_ref)):
+        total = parts[0].astype(f32)
+        for q in range(1, parts.shape[0]):
+            total += parts[q].astype(f32)
+        ref[0] = total
+
+
+def finish(experts, width, sums, gwi, gwd):
+    groups, part_rows, hidden = gwi.shape
+    height = sums.shape[0]
+    steps = 4 if part_rows % 64 == 0 else 1
+    piece = part_rows // steps
+    parts = pl.BlockSpec((groups, piece, hidden), lambda i: (0, i, 0))
+    whole = pl.BlockSpec((1, piece, hidden), lambda i: (0, i, 0))
+    qkv, out, router, gain_one, gain_two, gwi, gwd = pl.pallas_call(
+        finish_kernel,
+        grid=(steps,),
+        out_shape=(
+            Shape((height, 3 * width), f32),
+            Shape((height, width), f32),
+            Shape((height, experts), f32),
+            Shape((1, height), f32),
+            Shape((1, height), f32),
+            Shape((1, part_rows, hidden), f32),
+            Shape((1, part_rows, hidden), f32),
+        ),
+        in_specs=[fixed(*sums.shape), parts, parts],
+        out_specs=(
+            fixed(height, 3 * width),
+            fixed(height, width),
+            fixed(height, experts),
+            fixed(1, height),
+            fixed(1, height),
+            whole,
+            whole,
+        ),
+        compiler_params=pltpu.CompilerParams(vmem_limit_bytes=VMEM_LIMIT),
+    )(sums, gwi, gwd)
+    return qkv, out, router, gain_one.reshape(height), gain_two.reshape(height), gwi, gwd
+
+
 def body(
     lay, tokens, w_qkv, w_attn_out, w_router, gain_attn, gain_moe, w_expert_in, w_expert_down, key_mask,
     expert_choice, slot_index, cotangent,
@@ -783,41 +885,31 @@
     lane = jnp.arange(LANES, dtype=jnp.int32)[None, :]
     rest = jnp.pad(w_router, ((0, 0), (0, LANES - experts)))
     rest = jnp.where(lane == GAIN_LANE, gain_attn[:, None], jnp.where(lane == GAIN_LANE + 1, gain_moe[:, None], rest))
-    own = jnp.concatenate([w_qkv, w_attn_out, rest], axis=1)
+    own = [w_qkv, w_attn_out, rest]
     few = w_qkv.shape[0] % 16 != 0
     if few:
-        own = lax.all_gather(own, "seq", axis=0, tiled=True)
+        own = [lax.all_gather(part, "seq", axis=0, tiled=True) for part in own]
     rows = Rows(N, 1 if few else S)
 
     mask = lax.dynamic_slice_in_dim(key_mask, s * images, images, axis=0)
     mask = jnp.pad(mask, ((0, 0), (0, height - positions)))[:, None, :]
-    group, local = expert_choice // L, lax.rem(expert_choice, L)
+    choice, slot = expert_choice.transpose(0, 2, 1), slot_index.transpose(0, 2, 1)
+    group, local = choice // L, lax.rem(choice, L)
     member = local * S + lax.rem(group - g - local + (L + 1) * S, S)
-    code = jnp.where(slot_index >= 0, member * capacity + slot_index, -1)
-    code = jnp.pad(code, ((0, 0), (0, height - positions), (0, 0)), constant_values=-1)
-    code_rows = code.reshape(images * height, 2).T
+    code = jnp.where(slot >= 0, member * capacity + slot, -1)
+    code = jnp.pad(code, ((0, 0), (0, 0), (0, height - positions)), constant_values=-1)
+    code_rows = code.transpose(1, 0, 2).reshape(2, images * height)
 
     pack, gains, qkv, att, res, lse, routed, probs, gx, zy, gate, gwi, gwd = front(
         lay, rows, experts, capacity, own, tokens, mask, cotangent, code_rows, w_expert_in, w_expert_down
     )
     gtok, mixed, sums, gwi, gwd = back(
-        lay, rows, own.shape[0], tokens, mask, cotangent, code, qkv, att, res, lse, routed, probs, pack, gains, gx,
+        lay, rows, own[0].shape[0], tokens, mask, cotangent, code, qkv, att, res, lse, routed, probs, pack, gains, gx,
         gate, zy, gwi, gwd,
     )
     if few:
         sums = lax.psum_scatter(sums, "seq", scatter_dimension=0, tiled=True)
-    rest = sums[:, 4 * width :]
-    return (
-        mixed,
-        gtok,
-        sums[:, : 3 * width],
-        sums[:, 3 * width : 4 * width],
-        rest[:, :experts],
-        rest[:, GAIN_LANE],
-        rest[:, GAIN_LANE + 1],
-        jnp.sum(gwi.astype(f32), axis=0, keepdims=True),
-        jnp.sum(gwd.astype(f32), axis=0, keepdims=True),
-    )
+    return (mixed, gtok, *finish(experts, width, sums, gwi, gwd))
 
 
 def solution(mesh):

time: 420 us -> 361 us (0.86)
  Pallas kernels: 394 us -> 351 us
  local copies, waits for them, and re-layouts: 14.3 us -> 6.16 us
  other arithmetic: 10 us -> 2.19 us
    pallas_call x1, Pallas kernels: 150 us -> 123 us  [back(): pl.pallas_call(functools.partial(back_kernel, lay, rows), grid=(images,),...]
    pallas_call x1, Pallas kernels: 245 us -> 223 us  [front(): pl.pallas_call(functools.partial(front_kernel, lay, rows, experts), grid=...]
    slice x4 -> x0, local copies, waits for them, and re-layouts: 5.68 us -> none  [the longest x1 1.54 us: body(): sums[:, :3 * width]]
    reduce_sum x2 -> x0, other arithmetic: 5.45 us -> none  [the longest x1 3.68 us: body(): jnp.sum(gwi.astype(f32), axis=0, keepdims=True)]
    pallas_call x0 -> x1, Pallas kernels: none -> 4.93 us  [finish(): pl.pallas_call(finish_kernel, grid=(steps,), out_shape=(Shape((height, 3...]
where the time goes in v3:
time: 361 us
  Pallas kernels  351 us (97%)
  local copies, waits for them, and re-layouts  6.16 us (2%)
    pallas_call x1, Pallas kernels, front(): pl.pallas_call(functools.partial(front_kernel, lay, rows, experts), grid=...  223 us
    pallas_call x1, Pallas kernels, back(): pl.pallas_call(functools.partial(back_kernel, lay, rows), grid=(images,),...  123 us

profile of v3, /device:TPU:0, one launch (start us, length us, event | category | flops | bytes accessed | tf_op | source)
XLA Modules:
  0.0 360.5 jit_solution(3213711300639028897)
XLA Ops:
  0.6 0.0 copy-start
  0.7 1.4 select_select_fusion.own_refs_2_
  2.1 0.0 copy-done
  2.1 0.6 broadcast_in_dim.34.mask_ref
  2.7 0.8 compare_select_fusion.2
  3.5 0.6 pad_bitcast_fusion
  4.1 0.7 reshape.39.code_ref
  4.8 223.2 %shard_map.187 = (bf16[512,2176]{1,0:T(8,128)(2,1)}, f32[8,512]{1,0:T(8,128)}, bf16[8,208,1536]{2,1,0:T(8,128)(2,1)}, bf16[8,208,512]{2,1,0:T(8,128)(2,1)}, f32[...) custom-call(bf16[16,1536]{1,0:T(8,128)(2,1)} %own_refs_0_.1, ...), custom_call_target="tpu_custom_call" | custom-call | tf_op jit(solution)/shard_map/pallas_call | solution.py:457
  228.0 123.3 %shard_map.188 = (f32[8,200,512]{2,1,0:T(8,128)}, bf16[8,200,512]{2,1,0:T(8,128)(2,1)}, f32[16,2176]{1,0:T(8,128)}, bf16[2,256,2048]{2,1,0:T(8,128)(2,1)}, bf16[2,256,2048]{2,1,0:T(8,128)(2,1)}) custom-call(bf16[8,200,512]{2,1,0:T(8,128)(2,1)} %tok_ref.3, s32[8,1,208]{2,1,0:T(1,128)} %broadcast_in_dim.34.mask_ref, bf16[8,200,512]{2,1,0:T(8,128)(2,1)} %cot_ref.3, ...), custom_call_target="tpu_custom_call" | custom-call | tf_op jit(solution)/shard_map/pallas_call | solution.py:758
  351.4 0.0 copy-start.2
  351.4 4.9 %shard_map.189 = (f32[16,1536]{1,0:T(8,128)}, f32[16,512]{1,0:T(8,128)}, f32[16,16]{1,0:T(8,128)}, f32[1,16]{1,0:T(1,128)}, f32[1,16]{1,0:T(1,128)}, /*index=5*/f32[1,256,2048]{2,1,0:T(8,128)}, f32[1,256,2048]{2,1,0:T(8,128)}) custom-call(f32[16,2176]{1,0:T(8,128)} %get-tuple-element.49.sums_ref, bf16[2,256,2048]{2,1,0:T(8,128)(2,1)} %get-tuple-element.50.gwi_parts, ...), custom_call_target="tpu_custom_call" | custom-call | tf_op jit(solution)/shard_map/pallas_call | solution.py:846
  356.3 0.0 copy-start.1
  356.3 0.0 copy-done.2
  356.3 1.2 copy.24
  357.5 1.3 copy-done.1
  358.8 1.7 copy.25
  (4 shorter events, 0.0 us)
Async XLA Ops:
  0.6 1.4 copy-start
  351.4 4.9 %copy-start.2 = (bf16[8,200,512]{2,1,0:T(8,128)(2,1)S(1)}, bf16[8,200,512]{2,1,0:T(8,128)(2,1)}, u32[]{:S(2)}) copy-start(bf16[8,200,512]{2,1,0:T(8,128)(2,1)} %get-tuple-element.72) | copy-start | bytes 4915204
  356.3 2.5 copy-start.1

commit v4 on v3

--- a/solution.py
+++ b/solution.py
@@ -17,6 +17,7 @@
 TN = (((0,), (0,)), ((), ()))
 LANES = 128
 GAIN_LANE = 64
+LATE = 2
 VMEM_LIMIT = 60 << 20
 Shape = jax.ShapeDtypeStruct
 
@@ -122,10 +123,11 @@
         return lax.rem(g + s + l, self.S) * self.L + l
 
 
-def greet(peers):
+def greet(peers, meanwhile):
     barrier = pltpu.get_barrier_semaphore()
     for peer in peers:
         pl.semaphore_signal(barrier, inc=1, device_id=peer, device_id_type=MESH)
+    meanwhile()
     pl.semaphore_wait(barrier, len(peers))
 
 
@@ -154,9 +156,9 @@
                 yield i, q // self.S, lax.rem(q, self.S), lax.rem(q, self.S)
 
 
-def attend(heads, qkv, keep, width):
+def attend(heads, qkv, keep, width, soft_ref):
     head = width // heads
-    outs, lses = [], []
+    outs = []
     for h in range(heads):
         q = qkv[:, h * head : (h + 1) * head]
         k = qkv[:, width + h * head : width + (h + 1) * head]
@@ -165,15 +167,16 @@
         row_max = jnp.max(scores, axis=1, keepdims=True)
         exps = jnp.exp(scores - row_max)
         totals = jnp.sum(exps, axis=1, keepdims=True)
-        lses.append(row_max + jnp.log(totals))
-        outs.append(dot((exps / totals).astype(bf16), v).astype(bf16))
-    return jnp.concatenate(outs, axis=1), jnp.concatenate(lses, axis=1)
+        soft = (exps / totals).astype(bf16)
+        soft_ref[0, h] = soft
+        outs.append(dot(soft, v).astype(bf16))
+    return jnp.concatenate(outs, axis=1)
 
 
 def front_kernel(
     lay, rows, experts,
     own_refs, tok_ref, mask_ref, cot_ref, code_ref, w_in_ref, w_down_ref,
-    pack_ref, gains_ref, qkv_ref, att_ref, res_ref, lse_ref, routed_ref, probs_ref,
+    pack_ref, gains_ref, qkv_ref, att_ref, res_ref, soft_ref, routed_ref, probs_ref,
     gx_ref, zy_ref, gate_ref, gwi_ref, gwd_ref,
     own, full, routed, cot, w_in, w_down, x_send, c_send, x_recv, c_recv, gate_send, gwi, gwd,
     ps, pr, ws, wr, xs, xr, cs, cr, gs, gr, ts, tr, zs, ls,
@@ -246,19 +249,24 @@
 
     @pl.when(step == 0)
     def _():
+        def prepare():
+            first = 0
+            for ref in own_refs:
+                own[:, first : first + ref.shape[1]] = ref[...]
+                first += ref.shape[1]
+            for i in range(images):
+                cot[i] = pad_rows(cot_ref[i].astype(f32), height).astype(bf16)
+
         greet(
             [rows.device(i, b, c, s) for _, i in rows.along_a()]
             + [rows.device(a, b2, c, s2) for _, b2, s2, _ in rows.plane()]
             + [rows.device(a, b, 1 - c, s)]
             + lay.group_peers()
-            + lay.weight_peers()
+            + lay.weight_peers(),
+            prepare,
         )
         A, Q = rows.A, 2 * rows.S
         sl = s if rows.S > 1 else 0
-        first = 0
-        for ref in own_refs:
-            own[:, first : first + ref.shape[1]] = ref[...]
-            first += ref.shape[1]
         third = members // 3
         order = lay.order()
         pieces = part_rows // piece_rows
@@ -284,8 +292,6 @@
         ]
         for copy in copies:
             copy.start()
-        for i in range(images):
-            cot[i] = pad_rows(cot_ref[i].astype(f32), height).astype(bf16)
         build_c(0, third)
         local.wait()
         for copy in copies:
@@ -323,9 +329,8 @@
     normed = (hat * gains_ref[0:1, :]).astype(bf16)
     qkv = dot(normed, pack_ref[:, 0 : 3 * width]).astype(bf16)
     qkv_ref[0] = qkv
-    att, lse = attend(HEADS, qkv, mask_ref[0] > 0, width)
+    att = attend(HEADS, qkv, mask_ref[0] > 0, width, soft_ref)
     att_ref[0] = att
-    lse_ref[0] = lse
     residual = inputs + dot(att, pack_ref[:, 3 * width : 4 * width])
     res_ref[0] = residual
     hat, _ = norm_rows(residual)
@@ -339,7 +344,6 @@
         def dispatch(i, carry):
             k = lay.nth(i)
             pick_rows(jnp.bitwise_xor(me, k), routed, x_send)
-            x_copy(k).start()
             return carry
 
         lax.fori_loop(1, members, dispatch, 0)
@@ -361,6 +365,9 @@
                 @pl.when((delta != 0) | (s != p))
                 def _():
                     remote(src, dst, ws.at[0], wr.at[2 * p + copy_in], (0, 0)).wait_recv()
+
+        for k in lay.order():
+            x_copy(k).start()
 
         mine = lay.expert_of(g, me)
         hidden = w_in.shape[1]
@@ -463,7 +470,7 @@
             Shape((images, height, 3 * width), bf16),
             Shape((images, height, width), bf16),
             Shape((images, height, width), f32),
-            Shape((images, height, HEADS), f32),
+            Shape((images, HEADS, height, height), bf16),
             Shape((images, height, width), bf16),
             Shape((images, height, LANES), f32),
             Shape(blocks, bf16),
@@ -487,7 +494,7 @@
             per_image(height, 3 * width),
             per_image(height, width),
             per_image(height, width),
-            per_image(height, HEADS),
+            per_image(HEADS, height, height),
             per_image(height, width),
             per_image(height, LANES),
             anywhere(),
@@ -519,7 +526,7 @@
 
 def back_kernel(
     lay, rows,
-    tok_ref, mask_ref, cot_ref, code_ref, qkv_ref, att_ref, res_ref, lse_ref, routed_ref, probs_ref,
+    tok_ref, cot_ref, code_ref, qkv_ref, att_ref, res_ref, soft_ref, routed_ref, probs_ref,
     pack_ref, gains_ref, gx_ref, gate_ref, zy_ref, gwi_ref, gwd_ref,
     gtok_ref, mixed_ref, own_ref, gwi_parts, gwd_parts,
     gqkv, gout, grest, table, ggain, residuals, codes, zy, part, recv1, sum1, recv2, sum2, recv3,
@@ -574,20 +581,26 @@
 
     @pl.when(step == 0)
     def _():
+        def prepare():
+            for ref in (gqkv, gout, grest, ggain):
+                ref[...] = jnp.zeros_like(ref)
+            for m in range(members):
+                values = gate_ref[m].T[:, 0:1]
+                high = values.astype(bf16).astype(f32)
+                lane = lax.broadcasted_iota(jnp.int32, (cap, LANES), 1)
+                here = lane == lay.expert_of(g, jnp.int32(m))
+                span = slice(m * cap, (m + 1) * cap)
+                table[span, 0:LANES] = jnp.where(here, high, 0.0).astype(bf16)
+                table[span, LANES : 2 * LANES] = jnp.where(here, values - high, 0.0).astype(bf16)
+
         greet(
             [rows.device(i, b, c, s) for _, i in rows.along_a()]
             + [rows.device(a, b2, c, s2) for _, b2, s2, _ in rows.plane()]
             + [rows.device(a, b, 1 - c, s)]
             + lay.group_peers()
-            + lay.weight_peers()
+            + lay.weight_peers(),
+            prepare,
         )
-        pieces = part_rows // piece_rows
-        todo = [(p, q) for q in range(pieces) for p in range(S)]
-        order = lay.order()
-        for n, k in enumerate(order):
-            for p, q in todo[n * len(todo) // len(order) : (n + 1) * len(todo) // len(order)]:
-                weight_pieces(p, q)
-            zy_copy(k).start()
         zy_keep.start()
         for p in range(S):
 
@@ -596,19 +609,22 @@
                 for copy in weight_local(p):
                     copy.start()
 
-        for ref in (gqkv, gout, grest, ggain):
-            ref[...] = jnp.zeros_like(ref)
-        for m in range(members):
-            values = gate_ref[m].T[:, 0:1]
-            high = values.astype(bf16).astype(f32)
-            lane = lax.broadcasted_iota(jnp.int32, (cap, LANES), 1)
-            here = lane == lay.expert_of(g, jnp.int32(m))
-            span = slice(m * cap, (m + 1) * cap)
-            table[span, 0:LANES] = jnp.where(here, high, 0.0).astype(bf16)
-            table[span, LANES : 2 * LANES] = jnp.where(here, values - high, 0.0).astype(bf16)
+    order = lay.order()
+    todo = [(p, q) for q in range(part_rows // piece_rows) for p in range(S)]
+    count = residuals.shape[0]
+    turns = count + LATE
+
+    def background(turn):
+        for n in range(turn * len(todo) // turns, (turn + 1) * len(todo) // turns):
+            weight_pieces(*todo[n])
+        for k in order[2 * turn * len(order) // count : 2 * (turn + 1) * len(order) // count]:
+            zy_copy(k).start()
+
+    for turn in range(count):
+        pl.when(step == turn)(functools.partial(background, turn))
 
     def pick_slots(code):
-        slot = lax.broadcasted_iota(jnp.int32, (height, slots), 1)
+        slot = lax.broadcasted_iota(jnp.int32, (code.shape[0], slots), 1)
         return jnp.where((code[:, 0:1] == slot) | (code[:, 1:2] == slot), 1.0, 0.0).astype(bf16)
 
     wide = jnp.concatenate([code_ref[0].astype(f32), jnp.zeros((6, height), f32)], axis=0)
@@ -634,8 +650,7 @@
     grad_att = grad_residual.astype(bf16)
     gout[...] += dot(att_ref[0], grad_att, TN)
     grad_attended = dot(grad_att, pack_ref[:, 3 * width : 4 * width], NT).astype(bf16)
-    keep = mask_ref[0] > 0
-    qkv, lse = qkv_ref[0], lse_ref[0]
+    qkv, att = qkv_ref[0], att_ref[0]
     scale = head**-0.5
     grad_q, grad_k, grad_v = [], [], []
     for h in range(HEADS):
@@ -643,12 +658,10 @@
         k = qkv[:, width + h * head : width + (h + 1) * head]
         v = qkv[:, 2 * width + h * head : 2 * width + (h + 1) * head]
         ga = grad_attended[:, h * head : (h + 1) * head]
-        scores = jnp.where(keep, dot(q, k, NT) * scale, NEGATIVE)
-        weights = jnp.exp(scores - lse[:, h : h + 1])
-        grad_v.append(dot(weights.astype(bf16), ga, TN).astype(bf16))
-        grad_weights = dot(ga, v, NT)
-        row = jnp.sum(weights * grad_weights, axis=1, keepdims=True)
-        grad_scores = (weights * (grad_weights - row)).astype(bf16)
+        soft = soft_ref[0, h]
+        grad_v.append(dot(soft, ga, TN).astype(bf16))
+        row = jnp.sum(ga.astype(f32) * att[:, h * head : (h + 1) * head].astype(f32), axis=1, keepdims=True)
+        grad_scores = (soft.astype(f32) * (dot(ga, v, NT) - row)).astype(bf16)
         grad_q.append((dot(grad_scores, k) * scale).astype(bf16))
         grad_k.append((dot(grad_scores, q, TN) * scale).astype(bf16))
     grad_qkv = jnp.concatenate(grad_q + grad_k + grad_v, axis=1)
@@ -672,6 +685,7 @@
         part[..., 4 * width :] = grest[...].astype(bf16).reshape(shape + (LANES,))
         first = remote(part.at[:, :, 1 - c], recv1, ps.at[0], pr.at[0], rows.device(a, b, 1 - c, s))
         first.start()
+        background(count)
 
         def wait_zy(k, carry):
             zy_copy(k).wait()
@@ -680,15 +694,19 @@
         lax.fori_loop(1, members, wait_zy, 0)
         zy_keep.wait()
 
+        pair = 1 if residuals.shape[0] % 8 else 2
+
         def mix(first_image, last_image):
             def one(i, carry):
-                mixed = residuals[i] + dot(pick_slots(codes[i]), zy[...].reshape(slots, width))
-                mixed_ref[i] = mixed[:positions].astype(bf16)
+                chosen = pl.ds(i * pair, pair)
+                pick = pick_slots(codes[chosen].reshape(pair * height, 8))
+                mixed = residuals[chosen].reshape(pair * height, width) + dot(pick, zy[...].reshape(slots, width))
+                for n in range(pair):
+                    mixed_ref[i * pair + n] = mixed[n * height : n * height + positions].astype(bf16)
                 return carry
 
-            lax.fori_loop(first_image, last_image, one, 0)
-
-        count = residuals.shape[0]
+            lax.fori_loop(first_image // pair, last_image // pair, one, 0)
+
         mix(0, count // 4)
         first.wait()
         sum1[...] = (part[:, :, c].astype(f32) + recv1[...].astype(f32)).astype(bf16)
@@ -698,6 +716,7 @@
         ]
         for copy in copies:
             copy.start()
+        background(count + 1)
         mix(count // 4, count * 3 // 4)
         for copy in copies:
             copy.wait()
@@ -712,6 +731,8 @@
         ]
         for copy in copies:
             copy.start()
+        for turn in range(count + 2, turns):
+            background(turn)
         mix(count * 3 // 4, count)
         for copy in copies:
             copy.wait()
@@ -741,7 +762,7 @@
 
 
 def back(
-    lay, rows, own_height, tokens, mask, cotangent, code, qkv, att, res, lse, routed, probs, pack, gains, gx, gate,
+    lay, rows, own_height, tokens, cotangent, code, qkv, att, res, soft, routed, probs, pack, gains, gx, gate,
     zy, gwi, gwd,
 ):
     images, positions, width = tokens.shape
@@ -767,13 +788,12 @@
         ),
         in_specs=[
             per_image(positions, width),
-            per_image(1, height),
             per_image(positions, width),
             per_image(2, height),
             per_image(height, 3 * width),
             per_image(height, width),
             per_image(height, width),
-            per_image(height, HEADS),
+            per_image(HEADS, height, height),
             per_image(height, width),
             per_image(height, LANES),
             fixed(*pack.shape),
@@ -811,7 +831,7 @@
         compiler_params=pltpu.CompilerParams(
             collective_id=1, has_side_effects=True, vmem_limit_bytes=VMEM_LIMIT, dimension_semantics=("arbitrary",)
         ),
-    )(tokens, mask, cotangent, code, qkv, att, res, lse, routed, probs, pack, gains, gx, gate, zy, gwi, gwd)
+    )(tokens, cotangent, code, qkv, att, res, soft, routed, probs, pack, gains, gx, gate, zy, gwi, gwd)
 
 
 def finish_kernel(sums_ref, gwi_parts, gwd_parts, qkv_ref, out_ref, router_ref, gain_one, gain_two, gwi_ref, gwd_ref):
@@ -900,11 +920,11 @@
     code = jnp.pad(code, ((0, 0), (0, 0), (0, height - positions)), constant_values=-1)
     code_rows = code.transpose(1, 0, 2).reshape(2, images * height)
 
-    pack, gains, qkv, att, res, lse, routed, probs, gx, zy, gate, gwi, gwd = front(
+    pack, gains, qkv, att, res, soft, routed, probs, gx, zy, gate, gwi, gwd = front(
         lay, rows, experts, capacity, own, tokens, mask, cotangent, code_rows, w_expert_in, w_expert_down
     )
     gtok, mixed, sums, gwi, gwd = back(
-        lay, rows, own[0].shape[0], tokens, mask, cotangent, code, qkv, att, res, lse, routed, probs, pack, gains, gx,
+        lay, rows, own[0].shape[0], tokens, cotangent, code, qkv, att, res, soft, routed, probs, pack, gains, gx,
         gate, zy, gwi, gwd,
     )
     if few:

time: 361 us -> 354 us (0.981)
  Pallas kernels: 351 us -> 344 us
    pallas_call x1, Pallas kernels: 123 us -> 118 us  [back(): pl.pallas_call(functools.partial(back_kernel, lay, rows), grid=(images,),...]
where the time goes in v4:
time: 354 us; the launch traced here: 353 us
  Pallas kernels  344 us (97%)
  local copies, waits for them, and re-layouts  6.16 us (2%)
    pallas_call x1, Pallas kernels, front(): pl.pallas_call(functools.partial(front_kernel, lay, rows, experts), grid=...  220 us
    pallas_call x1, Pallas kernels, back(): pl.pallas_call(functools.partial(back_kernel, lay, rows), grid=(images,),...  118 us

profile of v4, /device:TPU:0, one launch (start us, length us, event | category | flops | bytes accessed | tf_op | source)
XLA Modules:
  0.0 352.7 jit_solution(7948260862733541771)
XLA Ops:
  0.6 0.0 copy-start
  0.7 1.4 select_select_fusion.own_refs_2_
  2.1 0.0 copy-done
  2.1 0.6 broadcast_in_dim.38.mask_ref
  2.7 0.8 compare_select_fusion.2
  3.5 0.6 pad_bitcast_fusion
  4.1 0.7 reshape.39.code_ref
  4.8 220.5 %shard_map.187 = (bf16[512,2176]{1,0:T(8,128)(2,1)}, f32[8,512]{1,0:T(8,128)}, bf16[8,208,1536]{2,1,0:T(8,128)(2,1)}, bf16[8,208,512]{2,1,0:T(8,128)(2,1)}, f32[...) custom-call(bf16[16,1536]{1,0:T(8,128)(2,1)} %own_refs_0_.1, ...), custom_call_target="tpu_custom_call" | custom-call | tf_op jit(solution)/shard_map/pallas_call | solution.py:464
  225.3 118.3 %shard_map.188 = (f32[8,200,512]{2,1,0:T(8,128)}, bf16[8,200,512]{2,1,0:T(8,128)(2,1)}, f32[16,2176]{1,0:T(8,128)}, bf16[2,256,2048]{2,1,0:T(8,128)(2,1)}, bf16[2,256,2048]{2,1,0:T(8,128)(2,1)}) custom-call(bf16[8,200,512]{2,1,0:T(8,128)(2,1)} %tok_ref.3, bf16[8,200,512]{2,1,0:T(8,128)(2,1)} %cot_ref.3, s32[8,2,208]{2,1,0:T(2,128)} %get-tuple-element.60.code_ref, ...), custom_call_target="tpu_custom_call" | custom-call | tf_op jit(solution)/shard_map/pallas_call | solution.py:779
  343.6 0.0 copy-start.2
  343.6 4.9 %shard_map.189 = (f32[16,1536]{1,0:T(8,128)}, f32[16,512]{1,0:T(8,128)}, f32[16,16]{1,0:T(8,128)}, f32[1,16]{1,0:T(1,128)}, f32[1,16]{1,0:T(1,128)}, /*index=5*/f32[1,256,2048]{2,1,0:T(8,128)}, f32[1,256,2048]{2,1,0:T(8,128)}) custom-call(f32[16,2176]{1,0:T(8,128)} %get-tuple-element.49.sums_ref, bf16[2,256,2048]{2,1,0:T(8,128)(2,1)} %get-tuple-element.50.gwi_parts, ...), custom_call_target="tpu_custom_call" | custom-call | tf_op jit(solution)/shard_map/pallas_call | solution.py:866
  348.5 0.0 copy-start.1
  348.5 0.0 copy-done.2
  348.5 1.2 copy.24
  349.7 1.3 copy-done.1
  351.0 1.7 copy.25
  (4 shorter events, 0.0 us)
Async XLA Ops:
  0.6 1.4 copy-start
  343.6 4.9 %copy-start.2 = (bf16[8,200,512]{2,1,0:T(8,128)(2,1)S(1)}, bf16[8,200,512]{2,1,0:T(8,128)(2,1)}, u32[]{:S(2)}) copy-start(bf16[8,200,512]{2,1,0:T(8,128)(2,1)} %get-tuple-element.72) | copy-start | bytes 4915204
  348.5 2.5 copy-start.1

commit v5 on v4

--- a/solution.py
+++ b/solution.py
@@ -178,8 +178,8 @@
     own_refs, tok_ref, mask_ref, cot_ref, code_ref, w_in_ref, w_down_ref,
     pack_ref, gains_ref, qkv_ref, att_ref, res_ref, soft_ref, routed_ref, probs_ref,
     gx_ref, zy_ref, gate_ref, gwi_ref, gwd_ref,
-    own, full, routed, cot, w_in, w_down, x_send, c_send, x_recv, c_recv, gate_send, gwi, gwd,
-    ps, pr, ws, wr, xs, xr, cs, cr, gs, gr, ts, tr, zs, ls,
+    own, full, routed, cot, w_in, w_down, x_send, c_send, x_recv, c_recv, gate_send, gwi, gwd, gwi_half, gwd_half,
+    ps, pr, ws, wr, xs, xr, cs, cr, gs, gr, ts, tr, zs, ls, os,
 ):
     step = pl.program_id(0)
     steps = pl.num_programs(0)
@@ -427,10 +427,10 @@
         ]
         for keep in keeps:
             keep.start()
-        gwi_ref[...] = gwi[...].astype(bf16)
-        gwd_ref[...] = gwd[...].astype(bf16)
-        for keep in keeps:
-            keep.wait()
+        for i, (total, half, ref) in enumerate(((gwi, gwi_half, gwi_ref), (gwd, gwd_half, gwd_ref))):
+            half[...] = total[...].astype(bf16)
+            keeps.append(pltpu.make_async_copy(half, ref, os.at[i]))
+            keeps[-1].start()
         zy_copy(0).wait()
         for d in range(1, S):
             for copy in weight_copies(d):
@@ -448,6 +448,8 @@
             return carry
 
         lax.fori_loop(1, members, finish, 0)
+        for keep in keeps:
+            keep.wait()
 
 
 def front(lay, rows, experts, cap, own, tokens, mask, cotangent, codes, w_in, w_down):
@@ -500,8 +502,8 @@
             anywhere(),
             anywhere(),
             anywhere(),
-            fixed(width, hidden),
-            fixed(width, hidden),
+            anywhere(),
+            anywhere(),
         ),
         scratch_shapes=[
             pltpu.VMEM(own_shape, bf16),
@@ -514,8 +516,11 @@
             pltpu.VMEM((M, 8, cap), f32),
             pltpu.VMEM((width, hidden), f32),
             pltpu.VMEM((width, hidden), f32),
+            pltpu.VMEM((width, hidden), bf16),
+            pltpu.VMEM((width, hidden), bf16),
             dma(count), dma(count), dma(2 * S), dma(2 * S),
             *[dma(M)] * 9,
+            dma(2),
             dma(2),
         ],
         compiler_params=pltpu.CompilerParams(

time: 354 us -> 352 us (level)
  no operation moved by 1% of the time
where the time goes in v5:
time: 352 us
  Pallas kernels  342 us (97%)
  local copies, waits for them, and re-layouts  6.16 us (2%)
    pallas_call x1, Pallas kernels, front(): pl.pallas_call(functools.partial(front_kernel, lay, rows, experts), grid=...  219 us
    pallas_call x1, Pallas kernels, back(): pl.pallas_call(functools.partial(back_kernel, lay, rows), grid=(images,),...  118 us

profile of v5, /device:TPU:0, one launch (start us, length us, event | category | flops | bytes accessed | tf_op | source)
XLA Modules:
  0.0 351.5 jit_solution(17184012750233980096)
XLA Ops:
  0.6 0.0 copy-start
  0.7 1.4 select_select_fusion.own_refs_2_
  2.1 0.0 copy-done
  2.1 0.6 broadcast_in_dim.38.mask_ref
  2.7 0.8 compare_select_fusion.2
  3.5 0.6 pad_bitcast_fusion
  4.1 0.7 reshape.39.code_ref
  4.8 219.3 %shard_map.187 = (bf16[512,2176]{1,0:T(8,128)(2,1)}, f32[8,512]{1,0:T(8,128)}, bf16[8,208,1536]{2,1,0:T(8,128)(2,1)}, bf16[8,208,512]{2,1,0:T(8,128)(2,1)}, f32[...) custom-call(bf16[16,1536]{1,0:T(8,128)(2,1)} %own_refs_0_.1, ...), custom_call_target="tpu_custom_call" | custom-call | tf_op jit(solution)/shard_map/pallas_call | solution.py:466
  224.1 118.3 %shard_map.188 = (f32[8,200,512]{2,1,0:T(8,128)}, bf16[8,200,512]{2,1,0:T(8,128)(2,1)}, f32[16,2176]{1,0:T(8,128)}, bf16[2,256,2048]{2,1,0:T(8,128)(2,1)}, bf16[2,256,2048]{2,1,0:T(8,128)(2,1)}) custom-call(bf16[8,200,512]{2,1,0:T(8,128)(2,1)} %tok_ref.3, bf16[8,200,512]{2,1,0:T(8,128)(2,1)} %cot_ref.3, s32[8,2,208]{2,1,0:T(2,128)} %get-tuple-element.60.code_ref, ...), custom_call_target="tpu_custom_call" | custom-call | tf_op jit(solution)/shard_map/pallas_call | solution.py:784
  342.4 0.0 copy-start.2
  342.4 4.9 %shard_map.189 = (f32[16,1536]{1,0:T(8,128)}, f32[16,512]{1,0:T(8,128)}, f32[16,16]{1,0:T(8,128)}, f32[1,16]{1,0:T(1,128)}, f32[1,16]{1,0:T(1,128)}, /*index=5*/f32[1,256,2048]{2,1,0:T(8,128)}, f32[1,256,2048]{2,1,0:T(8,128)}) custom-call(f32[16,2176]{1,0:T(8,128)} %get-tuple-element.49.sums_ref, bf16[2,256,2048]{2,1,0:T(8,128)(2,1)} %get-tuple-element.50.gwi_parts, ...), custom_call_target="tpu_custom_call" | custom-call | tf_op jit(solution)/shard_map/pallas_call | solution.py:871
  347.3 0.0 copy-start.1
  347.3 0.0 copy-done.2
  347.3 1.2 copy.24
  348.5 1.3 copy-done.1
  349.8 1.7 copy.25
  (4 shorter events, 0.0 us)
Async XLA Ops:
  0.6 1.4 copy-start
  342.4 4.9 %copy-start.2 = (bf16[8,200,512]{2,1,0:T(8,128)(2,1)S(1)}, bf16[8,200,512]{2,1,0:T(8,128)(2,1)}, u32[]{:S(2)}) copy-start(bf16[8,200,512]{2,1,0:T(8,128)(2,1)} %get-tuple-element.72) | copy-start | bytes 4915204
  347.3 2.5 copy-start.1
